TPU v7x, 128 devices: a whole 4x4x4 slice. The times are simulated.
128 devices in a mesh: grp: 32 (over x, y, core), exp: 4 (over z).
Axes of the slice: x: 4, y: 4, z: 4, core: 2. Of those that a mesh axis runs over, the one named last changes fastest.
Arguments:
- hidden_in: bfloat16 [16384, 7168], P(('grp', 'exp')), may hold values from -6 to 6
- weights: bfloat16 [114688, 4096], P(('grp', 'exp')), may hold values from -0.0625 to 0.0625
- gates: float32 [16384], P(('grp', 'exp')), may hold values from 0.1 to 1
- group_ids: int32 [16384], P(('grp', 'exp')), may hold values from 0 to 15, as said below
- slot_ids: int32 [16384], P(('grp', 'exp')), may hold values from 0 to 9, as said below
- out_grad: bfloat16 [16384, 4096], P(('grp', 'exp')), may hold values from -6 to 6
Outputs:
- mixed_out: bfloat16 [16384, 4096], P(('grp', 'exp'))
- hidden_grad: bfloat16 [16384, 7168], P(('grp', 'exp'))
- weight_grad: bfloat16 [114688, 4096], P(('grp', 'exp'))
- gate_grad: float32 [16384], P(('grp', 'exp'))
Inputs may be any that keep to these rules, and one draw needn't show every extreme that they name: `group_ids`: on each device at most 10 of its 128 tokens name one group, and on every device some group is named by exactly 10 tokens. `slot_ids`: tokens of one device that name the same group have distinct slots.
All inputs are finite; a program needn't handle non-finite values.
Results may differ from a plain program's by a relative error of at most 0.017.
Values may be sent and summed in bfloat16 or wider, within the bound.
A program may use at most 192 MiB of HBM per device.

v0:
```python
import jax
import jax.numpy as jnp
from jax import lax
from jax.sharding import PartitionSpec as P


def swapped(value, axis, stride):
    mask = 2**stride
    pairs = [(source, source ^ mask) for source in range(lax.axis_size(axis))]
    return lax.ppermute(value, axis, pairs)


def select_matrix(position, slots_total):
    return (jnp.arange(slots_total, dtype=jnp.int32)[:, None] == position[None, :]).astype(
        jnp.bfloat16
    )


def slots_to_tokens(picker, table):
    return lax.dot_general(
        picker, table, (((0,), (0,)), ((), ())), preferred_element_type=jnp.float32
    )


def local(hidden_in, weights, gates, group_ids, slot_ids, out_grad):
    tok_rows = hidden_in.shape[0]
    width_ff = hidden_in.shape[1]
    width_d = out_grad.shape[1]
    ff_block = weights.shape[0]
    n_grp = lax.axis_size("grp")
    n_exp = lax.axis_size("exp")
    n_groups = n_grp // 2
    capacity = tok_rows * 5 // (4 * n_groups)
    half_ff = width_ff // 2
    half_d = width_d // 2
    parity = lax.axis_index("grp") % 2
    position = group_ids * capacity + slot_ids
    picker = select_matrix(position, n_groups * capacity)
    halves = []
    for column_half in range(2):
        chosen = jnp.dot(
            picker,
            hidden_in[:, column_half * half_ff : (column_half + 1) * half_ff],
            preferred_element_type=jnp.float32,
        )
        halves.append(chosen.astype(jnp.bfloat16).reshape(n_groups, capacity, half_ff))
    packed = jnp.stack(halves, axis=1).reshape(n_grp, capacity, n_exp, ff_block)
    arrived = lax.all_to_all(
        lax.all_to_all(packed, "grp", split_axis=0, concat_axis=0, tiled=True),
        "exp",
        split_axis=2,
        concat_axis=0,
        tiled=True,
    )
    rows_in = arrived.reshape(-1, ff_block)
    partial_value = jnp.dot(rows_in, weights, preferred_element_type=jnp.float32)
    summed = lax.psum_scatter(
        lax.optimization_barrier(partial_value.astype(jnp.bfloat16))
        .astype(jnp.float32)
        .astype(jnp.bfloat16),
        "exp",
        scatter_dimension=0,
        tiled=True,
    ).astype(jnp.float32)
    own_half = lax.dynamic_slice_in_dim(summed, parity * half_d, half_d, 1)
    other_half = lax.dynamic_slice_in_dim(summed, (1 - parity) * half_d, half_d, 1)
    own_half = own_half + swapped(other_half.astype(jnp.bfloat16), "grp", 0).astype(
        other_half.dtype
    )
    expert_half = own_half.astype(jnp.bfloat16).reshape(n_grp, capacity, half_d)
    returned_rows = lax.all_to_all(expert_half, "grp", split_axis=0, concat_axis=0, tiled=True)
    expert_rows = (
        returned_rows.reshape(n_groups, 2, capacity, half_d)
        .transpose(0, 2, 1, 3)
        .reshape(n_groups * capacity, width_d)
    )
    picked = slots_to_tokens(picker, expert_rows)
    mixed_out = (gates[:, None] * picked).astype(jnp.bfloat16)
    gate_grad = jnp.sum(out_grad.astype(jnp.float32) * picked, axis=1)
    cotangent = (gates[:, None] * out_grad.astype(jnp.float32)).astype(jnp.bfloat16)
    cot_slots = (
        jnp.dot(picker, cotangent, preferred_element_type=jnp.float32)
        .astype(jnp.bfloat16)
        .reshape(n_groups, capacity, width_d)
    )
    split_cot = jnp.stack([cot_slots[:, :, :half_d], cot_slots[:, :, half_d:]], axis=1).reshape(
        n_grp, capacity, half_d
    )
    received = lax.all_to_all(split_cot, "grp", split_axis=0, concat_axis=0, tiled=True)
    mine_rows = lax.all_gather(received, "exp", axis=0, tiled=True).reshape(-1, half_d)
    other_rows = swapped(mine_rows, "grp", 0)
    low_half = jnp.where(parity == 0, mine_rows, other_rows)
    high_half = jnp.where(parity == 0, other_rows, mine_rows)
    cot_rows = jnp.concatenate([low_half, high_half], axis=1)
    hidden_part = lax.dot_general(
        cot_rows, weights, (((1,), (1,)), ((), ())), preferred_element_type=jnp.float32
    ).astype(jnp.bfloat16)
    weight_grad = lax.dot_general(
        rows_in, cot_rows, (((0,), (0,)), ((), ())), preferred_element_type=jnp.float32
    ).astype(jnp.bfloat16)
    grad_blocks = hidden_part.reshape(n_exp, n_grp, capacity, ff_block)
    grad_back = lax.all_to_all(
        lax.all_to_all(grad_blocks, "grp", split_axis=1, concat_axis=1, tiled=True),
        "exp",
        split_axis=0,
        concat_axis=0,
        tiled=True,
    )
    grad_slots = (
        grad_back.reshape(n_exp, n_groups, 2, capacity, ff_block)
        .transpose(1, 3, 2, 0, 4)
        .reshape(n_groups * capacity, width_ff)
    )
    hidden_grad = slots_to_tokens(picker, grad_slots).astype(jnp.bfloat16)
    return (mixed_out, hidden_grad, weight_grad, gate_grad)


def solution(mesh):
    placed = (
        P(("grp", "exp"), None),
        P(("grp", "exp"), None),
        P(("grp", "exp")),
        P(("grp", "exp")),
        P(("grp", "exp")),
        P(("grp", "exp"), None),
    )
    return jax.shard_map(
        local,
        mesh=mesh,
        in_specs=placed,
        out_specs=(
            P(("grp", "exp"), None),
            P(("grp", "exp"), None),
            P(("grp", "exp"), None),
            P(("grp", "exp")),
        ),
        check_vma=False,
    )
```

profile of v0, /device:TPU:1, one launch (start us, length us, event | category | flops | bytes accessed | tf_op | source)
XLA Modules:
  0.0 340.7 jit_solution(11287478807243527306)
XLA Ops:
  10.9 36.5 %all_to_all.40 = bf16[32,10,2048]{2,1,0:T(8,128)(2,1)S(1)} all-to-all(bf16[32,10,2048]{2,1,0:T(8,128)(2,1)S(1)} %bitcast.30), channel_id=1, replica_groups=mesh['grp'=32,'exp'=4] {'grp'}, dimensions={0} | all-to-all | bytes 2621440 | tf_op jit(solution)/shard_map/all_to_all | solution.py:89
  53.3 2.0 pad_maximum_fusion.3
  55.3 2.1 copy.38
  57.4 5.1 %reshape.55 = bf16[32,10,4,896]{3,2,1,0:T(4,128)(2,1)S(1)} reshape(bf16[16,2,10,3584]{3,2,1,0:T(8,128)(2,1)} %copy.38) | data formatting | bytes 4587520 | tf_op jit(solution)/shard_map/reshape | solution.py:47
  62.5 34.5 %all_to_all.41 = bf16[32,10,4,896]{3,2,1,0:T(4,128)(2,1)S(1)} all-to-all(bf16[32,10,4,896]{3,2,1,0:T(4,128)(2,1)S(1)} %reshape.55), channel_id=1, replica_groups=mesh['grp'=32,'exp'=4] {'grp'}, dimensions={0} | all-to-all | bytes 4587520 | tf_op jit(solution)/shard_map/all_to_all | solution.py:49
  97.3 32.7 %all_to_all.42 = bf16[32,10,4,896]{3,0,1,2:T(8,128)(2,1)S(1)} all-to-all(bf16[32,10,4,896]{3,0,1,2:T(8,128)(2,1)S(1)} %copy.28), channel_id=1, replica_groups=mesh['grp'=32,'exp'=4] {'exp'}, dimensions={2} | all-to-all | bytes 4587520 | tf_op jit(solution)/shard_map/all_to_all | solution.py:48
  130.0 2.8 copy.29
  132.8 3.9 %reshape.45 = bf16[1280,896]{1,0:T(8,128)(2,1)S(1)} reshape(bf16[4,32,10,1,896]{4,2,1,0,3:T(8,128)(2,1)} %copy.29) | data formatting | bytes 4587520 | tf_op jit(solution)/shard_map/reshape | solution.py:55
  136.7 17.0 %convolution_convert_fusion = bf16[1280,4096]{1,0:T(8,128)(2,1)} fusion(bf16[1280,896]{1,0:T(8,128)(2,1)S(1)} %reshape.45, bf16[896,4096]{1,0:T(8,128)(2,1)} %param.7), kind=kOutput, calls=%fused_computation | convolution fusion | flops 9400483840 | bytes 20119552 | tf_op jit(solution)/shard_map/dot_general | solution.py:56
  153.8 9.4 %copy.34 = bf16[128,10,2048]{2,1,0:T(8,128)(2,1)} copy(bf16[128,10,2048]{2,0,1:T(8,128)(2,1)} %all-gather.2.cloned.1.call-done) | data formatting | bytes 10485760 | tf_op jit(solution)/shard_map/all_gather | solution.py:90
  163.2 9.9 %reshape.51 = bf16[1280,2048]{1,0:T(8,128)(2,1)} reshape(bf16[128,10,2048]{2,1,0:T(8,128)(2,1)} %copy.34) | data formatting | bytes 10485760 | tf_op jit(solution)/shard_map/reshape | solution.py:90
  174.7 8.6 %collective-permute-done.1 = bf16[1280,2048]{1,0:T(8,128)(2,1)} collective-permute-done((bf16[1280,2048]{1,0:T(8,128)(2,1)}, bf16[1280,2048]{1,0:T(8,128)(2,1)}, u32[]{:S(2)}, u32[]{:S(2)}) %collective-permute-start.1) | collective-permute-done | bytes 5242912 | tf_op jit(solution)/shard_map/ppermute | solution.py:10
  183.3 8.8 %broadcast_select_fusion.1 = (bf16[1280,2048]{1,0:T(8,128)(2,1)}, bf16[1280,2048]{1,0:T(8,128)(2,1)}) fusion(bf16[1280,2048]{1,0:T(8,128)(2,1)} %reshape.51, bf16[1280,2048]{1,0:T(8,128)(2,1)} %collective-permute-done.1, pred[]{:T(512)S(6)} %eq.22), kind=kLoop, calls=%fused_computation.6 | loop fusion | flops 5242880 | bytes 20971520 | tf_op jit(solution)/shard_map/jit(_where)/select_n | solution.py:92
  192.1 15.8 %fusion.1 = bf16[1280,896]{1,0:T(8,128)(2,1)S(1)} fusion(bf16[896,4096]{1,0:T(8,128)(2,1)} %param.7, bf16[1280,2048]{1,0:T(8,128)(2,1)} %get-tuple-element.5, bf16[1280,2048]{1,0:T(8,128)(2,1)} %get-tuple-element.4), kind=kOutput, calls=%fused_computation.11 | convolution fusion | flops 9417359360 | bytes 20119552 | tf_op jit(solution)/shard_map/dot_general | solution.py:95
  207.9 2.5 reshape.52
  210.4 5.2 %copy.35 = bf16[4,32,10,896]{3,0,2,1:T(4,128)(2,1)} copy(bf16[4,32,10,896]{3,2,1,0:T(8,128)(2,1)} %reshape.52) | data formatting | bytes 4587520 | tf_op jit(solution)/shard_map/reshape | solution.py:101
  215.6 6.3 %all-to-all-start.4 = ((bf16[4,32,10,896]{3,0,2,1:T(4,128)(2,1)}), bf16[4,32,10,896]{3,0,2,1:T(4,128)(2,1)S(1)}, u32[]{:S(2)}, u32[]{:S(2)}) async-start(bf16[4,32,10,896]{3,0,2,1:T(4,128)(2,1)} %copy.35), calls=%async_computation.5 | async-start | bytes 4587520 | tf_op jit(solution)/shard_map/all_to_all | solution.py:103
  221.9 29.4 %reduce-scatter.2.cloned.1.call-done = bf16[320,4096]{1,0:T(8,128)(2,1)} async-done(((bf16[1280,4096]{1,0:T(8,128)(2,1)}), bf16[320,4096]{1,0:T(8,128)(2,1)}) %reduce-scatter.2.cloned.1.call-update) | async-done | bytes 2621456 | tf_op jit(solution)/shard_map/reduce_scatter | solution.py:57
  251.3 2.4 convert_element_type.49
  253.7 2.4 copy-done
  259.6 3.6 %all-to-all-start.5 = ((bf16[4,32,10,896]{3,1,2,0:T(8,128)(2,1)}), bf16[4,32,10,896]{3,1,2,0:T(8,128)(2,1)S(1)}, u32[]{:S(2)}, u32[]{:S(2)}) async-start(bf16[4,32,10,896]{3,1,2,0:T(8,128)(2,1)} %copy.36), calls=%async_computation.6 | async-start | bytes 4587520 | tf_op jit(solution)/shard_map/all_to_all | solution.py:102
  263.3 3.6 %add_convert_fusion = bf16[320,2048]{1,0:T(8,128)(2,1)} fusion(bf16[320,2048]{1,0:T(8,128)(2,1)} %collective-permute-done, f32[320,4096]{1,0:T(8,128)} %copy-done, s32[]{:T(128)S(6)} %select_n.26), kind=kLoop, calls=%fused_computation.14 | loop fusion | flops 1966080 | bytes 5242884 | tf_op jit(solution)/shard_map/convert_element_type | solution.py:70
  266.9 3.4 reshape.46
  270.3 21.6 %all-to-all-done.5 = bf16[4,32,10,896]{3,1,2,0:T(8,128)(2,1)S(1)} async-done(((bf16[4,32,10,896]{3,1,2,0:T(8,128)(2,1)}), bf16[4,32,10,896]{3,1,2,0:T(8,128)(2,1)S(1)}, u32[]{:S(2)}, u32[]{:S(2)}) %all-to-all-start.5) | async-done | bytes 2293792 | tf_op jit(solution)/shard_map/all_to_all | solution.py:102
  291.8 7.7 %all-to-all-start.2 = ((bf16[32,10,2048]{2,1,0:T(8,128)(2,1)}), bf16[32,10,2048]{2,1,0:T(8,128)(2,1)}, u32[]{:S(2)}, u32[]{:S(2)}) async-start(bf16[32,10,2048]{2,1,0:T(8,128)(2,1)} %reshape.46), calls=%async_computation.3 | async-start | bytes 4194304 | tf_op jit(solution)/shard_map/all_to_all | solution.py:71
  299.5 15.2 %convolution_convert_fusion.2 = bf16[896,4096]{1,0:T(8,128)(2,1)} fusion(bf16[1280,896]{1,0:T(8,128)(2,1)} %copy-done.2, bf16[1280,2048]{1,0:T(8,128)(2,1)} %get-tuple-element.5, bf16[1280,2048]{1,0:T(8,128)(2,1)} %get-tuple-element.4), kind=kOutput, calls=%fused_computation.3 | convolution fusion | flops 9419882496 | bytes 20119552 | tf_op jit(solution)/shard_map/dot_general | solution.py:98
  314.7 2.3 reshape.53
  317.0 4.6 %copy.44 = bf16[4,16,2,10,896]{4,0,2,3,1:T(4,128)(2,1)S(1)} copy(bf16[4,16,2,10,896]{4,2,1,3,0:T(2,128)(2,1)} %reshape.53) | data formatting | bytes 4587520 | tf_op jit(solution)/shard_map/reshape | solution.py:110
  321.6 2.9 reshape.54
  324.5 3.6 %convolution_convert_fusion.1 = bf16[128,7168]{1,0:T(8,128)(2,1)} fusion(bf16[160,7168]{1,0:T(8,128)(2,1)} %reshape.54, s32[128]{0:T(128)S(1)} %multiply_add_fusion), kind=kOutput, calls=%fused_computation.2 | convolution fusion | flops 294539264 | bytes 4129280 | tf_op jit(solution)/shard_map/dot_general | solution.py:20
  328.1 3.0 copy.30
  331.7 2.2 fusion.3
  (34 shorter events, 15.5 us)
Async XLA Ops:
  7.2 146.6 %all-gather.2.cloned.1.call-start = ((), (), s32[]{:S(2)}) async-start(), calls=%async_computation.8 | async-start | bytes 6553600 | tf_op jit(solution)/shard_map/all_gather | solution.py:90
  47.4 2.0 copy-start.3
  49.3 202.0 %reduce-scatter.2.cloned.1.call-start = ((), (), s32[]{:S(2)}) async-start(), calls=%async_computation.7 | async-start | bytes 13107200 | tf_op jit(solution)/shard_map/reduce_scatter | solution.py:57
  136.7 17.0 %copy-start.2 = (bf16[1280,896]{1,0:T(8,128)(2,1)}, bf16[1280,896]{1,0:T(8,128)(2,1)S(1)}, u32[]{:S(2)}) copy-start(bf16[1280,896]{1,0:T(8,128)(2,1)S(1)} %reshape.45) | copy-start | bytes 6881284
  173.2 10.2 %collective-permute-start.1 = (bf16[1280,2048]{1,0:T(8,128)(2,1)}, bf16[1280,2048]{1,0:T(8,128)(2,1)}, u32[]{:S(2)}, u32[]{:S(2)}) collective-permute-start(bf16[1280,2048]{1,0:T(8,128)(2,1)} %reshape.51), channel_id=1, source_target_pairs={{0,4},{4,0},{8,12},{12,8},{16,20},{20,16},{24,28},{28,24},{32,36},... | collective-permute-start | bytes 15728648 | tf_op jit(solution)/shard_map/ppermute | solution.py:10
  215.6 42.3 %all-to-all-start.4 = ((bf16[4,32,10,896]{3,0,2,1:T(4,128)(2,1)}), bf16[4,32,10,896]{3,0,2,1:T(4,128)(2,1)S(1)}, u32[]{:S(2)}, u32[]{:S(2)}) async-start(bf16[4,32,10,896]{3,0,2,1:T(4,128)(2,1)} %copy.35), calls=%async_computation.5 | async-start | bytes 4587520 | tf_op jit(solution)/shard_map/all_to_all | solution.py:103
  253.7 2.4 copy-start
  257.3 6.0 %collective-permute-start = (bf16[320,2048]{1,0:T(8,128)(2,1)}, bf16[320,2048]{1,0:T(8,128)(2,1)}, u32[]{:S(2)}, u32[]{:S(2)}) collective-permute-start(bf16[320,2048]{1,0:T(8,128)(2,1)} %dynamic-slice_convert_fusion), channel_id=1, source_target_pairs={{0,4},{4,0},{8,12},{12,8},{16,20},{20,16},{24,28},{28,24},{32,36},... | collective-permute-start | bytes 3932168 | tf_op jit(solution)/shard_map/ppermute | solution.py:10
  259.6 32.2 %all-to-all-start.5 = ((bf16[4,32,10,896]{3,1,2,0:T(8,128)(2,1)}), bf16[4,32,10,896]{3,1,2,0:T(8,128)(2,1)S(1)}, u32[]{:S(2)}, u32[]{:S(2)}) async-start(bf16[4,32,10,896]{3,1,2,0:T(8,128)(2,1)} %copy.36), calls=%async_computation.6 | async-start | bytes 4587520 | tf_op jit(solution)/shard_map/all_to_all | solution.py:102
  291.8 36.2 %all-to-all-start.2 = ((bf16[32,10,2048]{2,1,0:T(8,128)(2,1)}), bf16[32,10,2048]{2,1,0:T(8,128)(2,1)}, u32[]{:S(2)}, u32[]{:S(2)}) async-start(bf16[32,10,2048]{2,1,0:T(8,128)(2,1)} %reshape.46), calls=%async_computation.3 | async-start | bytes 4194304 | tf_op jit(solution)/shard_map/all_to_all | solution.py:71
  328.1 3.6 %copy-start.1 = (bf16[128,4096]{1,0:T(8,128)(2,1)S(1)}, bf16[128,4096]{1,0:T(8,128)(2,1)}, u32[]{:S(2)}) copy-start(bf16[128,4096]{1,0:T(8,128)(2,1)} %param.11) | copy-start | bytes 3145732
  328.1 3.6 %copy-start.4 = (f32[128]{0:T(128)S(1)}, f32[128]{0:T(128)}, u32[]{:S(2)}) copy-start(f32[128]{0:T(128)} %param.8) | copy-start | bytes 1540
Sparse Core Ops, SparseCore 0:
  49.4 55.7 all-gather.1
  153.9 97.3 reduce-scatter.1
where the time goes:
time: 342 us; the launch traced here: 341 us
  blocking collectives  104 us (30%)
  local copies, waits for them, and re-layouts  68 us (20%)
  waiting for transfers between devices  59.7 us (17%)
  matrix products  57.6 us (17%)
  starting transfers between devices  19.8 us (6%)
  other arithmetic  17.6 us (5%)
  between operations  14.3 us (4%)
    all_to_all x1, blocking collectives, local(): lax.all_to_all(split_cot, 'grp', split_axis=0, concat_axis=0, tiled=True)  36.5 us
    all_to_all x1, blocking collectives, local(): lax.all_to_all(packed, 'grp', split_axis=0, concat_axis=0, tiled=True)  34.5 us
    all_to_all x1, blocking collectives, local(): lax.all_to_all(lax.all_to_all(packed, 'grp', split_axis=0, concat_axis=0,...  32.7 us
    reduce_scatter x1, waiting for transfers between devices, local(): lax.psum_scatter(lax.optimization_barrier(partial_value.astype(jnp.bfloat...  29.4 us
    all_to_all x1, waiting for transfers between devices, local(): lax.all_to_all(lax.all_to_all(grad_blocks, 'grp', split_axis=1, concat_ax...  21.6 us
    dot_general x1, matrix products, local(): jnp.dot(rows_in, weights, preferred_element_type=jnp.float32)  17 us
    dot_general x1, matrix products, local(): lax.dot_general(cot_rows, weights, (((1,), (1,)), ((), ())), preferred_el...  15.8 us
    dot_general x1, matrix products, local(): lax.dot_general(rows_in, cot_rows, (((0,), (0,)), ((), ())), preferred_el...  15.2 us
  transfers between devices with their start and end apart: 7, of which 3 were waited for; matrix products, arithmetic and copies ran while one was open for 38% of the time, Pallas kernels for 0%

commit v1 on v0

v1 whole, which is shorter than its diff:
```python
import functools

import jax
import jax.numpy as jnp
from jax import lax
from jax.experimental import pallas as pl
from jax.experimental.pallas import tpu as pltpu
from jax.sharding import PartitionSpec as P

MESH = pl.DeviceIdType.MESH
BF = jnp.bfloat16
F32 = jnp.float32
TOK, CAP = 128, 10
D, FF, FB = 4096, 7168, 896
HD, QD, XD = D // 2, D // 4, D // 8
NP, NZ = 16, 4
MAIN, EXT, ROWS = 256, 64, 320


def hops(k):
    return min(k, 4 - k)


PLANE = sorted(
    [(i, j) for i in range(4) for j in range(4) if i + j], key=lambda o: -(hops(o[0]) + hops(o[1]))
)
COLUMN = [(0, 2), (1, 2), (0, 1), (0, 3), (1, 1), (1, 3), (1, 0)]


def dot(a, b, dims=((1,), (0,))):
    return lax.dot_general(a, b, (dims, ((), ())), preferred_element_type=F32)


def dot_tn(a, b):
    return dot(a, b, ((0,), (0,)))


def dot_nt(a, b):
    return dot(a, b, ((1,), (1,)))


def one(cond):
    return jnp.where(cond, 1.0, 0.0).astype(F32).astype(BF)


def iota(shape, dim):
    return lax.broadcasted_iota(jnp.int32, shape, dim)


def mult(value, of):
    return pl.multiple_of(value, of)


def kernel(
    hid, w_hbm, gates, pos, og_hbm,
    mixed, hg, wg, gg,
    wv, h, hxr, cot, cxp, xh, sm, sx, tok, tsend, gm, gx, pa, prcv, r1, r2, ex, em, exr, hp, hpx, rm, rx, kk, kr, og,
    mt, xb, posv,
    pos_s, pos_r, hz_s, hz_r, w_sem, og_sem, t_s, t_r, cm_s, cm_r, cx_s, cx_r, hm_s, hm_r,
    ag_s, ag_r, agf_s, agf_r, sib_s, sib_r, po_s, po_r, rs_s, rs_r, ret_s, ret_r, eo_s, eo_r, k_s, k_r, hg_s, hg_r, wg_sem,
):
    g = lax.axis_index("grp")
    z = lax.axis_index("exp")
    c = lax.rem(g, 2)
    p = lax.div(g, 2)
    x = lax.div(p, 4)
    y = lax.rem(p, 4)
    nc = 1 - c
    zp = lax.rem(z + 1, 4)
    zm = lax.rem(z + 3, 4)
    zo = lax.rem(z + 2, 4)
    sib = (p * 2 + nc, z)
    up = (g, zp)
    down = (g, zm)
    blk = c * 4 + z

    def plane(i, j):
        p2 = lax.rem(x + i, 4) * 4 + lax.rem(y + j, 4)
        return p2, (p2 * 2 + c, z)

    def column(dc, dz):
        c2 = lax.rem(c + dc, 2)
        z2 = lax.rem(z + dz, 4)
        return c2, z2, (p * 2 + c2, z2)

    def remote(src, dst, ss, rs, dev):
        return pltpu.make_async_remote_copy(
            src_ref=src, dst_ref=dst, send_sem=ss, recv_sem=rs, device_id=dev, device_id_type=MESH
        )

    def local(src, dst, sem):
        return pltpu.make_async_copy(src, dst, sem)

    def drain(ref, sem):
        pltpu.make_async_copy(ref, ref, sem).wait()

    def rows(ref, start, size, of=16):
        return ref.at[pl.ds(mult(start, of), size)]

    def cols(start, size):
        return pl.ds(mult(start, 128), size)

    local(og_hbm, og, og_sem.at[0]).start()
    local(w_hbm, wv, w_sem.at[0]).start()
    posv[pl.ds(mult((z * 2 + c) * 8, 8), 8), :] = pos[...]

    barrier = pltpu.get_barrier_semaphore()
    for dc, dz in COLUMN:
        pl.semaphore_signal(barrier, inc=1, device_id=column(dc, dz)[2], device_id_type=MESH)
    for i, j in PLANE:
        pl.semaphore_signal(barrier, inc=1, device_id=plane(i, j)[1], device_id_type=MESH)
    pl.semaphore_wait(barrier, len(COLUMN) + len(PLANE))

    mine = rows(posv, (z * 2 + c) * 8, 8, 8)
    for dc, dz in COLUMN:
        remote(mine, mine, pos_s.at[0], pos_r.at[0], column(dc, dz)[2]).start()

    def send_hidden(piece, _):
        for dc, dz in COLUMN:
            c2, z2, dev = column(dc, dz)
            src = hid.at[pl.ds(mult(piece * 32, 16), 32), cols((c2 * 4 + z2) * FB, FB)]
            dst = rows(xh, (z * 2 + c) * TOK + piece * 32, 32)
            remote(src, dst, hz_s.at[0], hz_r.at[0], dev).start()
        return 0

    lax.fori_loop(0, 4, send_hidden, 0)
    local(hid.at[:, cols(blk * FB, FB)], rows(xh, (z * 2 + c) * TOK, TOK), hz_r.at[0]).start()

    eye = iota((TOK, TOK), 0) == iota((TOK, TOK), 1)
    gate = jnp.sum(jnp.where(eye, gates[...], 0.0), axis=1, keepdims=True)
    drain(og, og_sem.at[0])
    tsend[...] = (gate * og[:, cols(nc * HD, HD)].astype(F32)).astype(BF)
    remote(tsend, rows(tok, c * TOK, TOK), t_s.at[0], t_r.at[0], sib).start()
    tok[pl.ds(mult(c * TOK, 16), TOK), :] = (gate * og[:, cols(c * HD, HD)].astype(F32)).astype(BF)

    drain(rows(posv, 0, 56, 8), pos_r.at[0])

    def tables(zz, _):
        group = iota((MAIN, TOK), 0) // 16
        slot = iota((MAIN, TOK), 0) % 16
        both = posv[pl.ds(mult(zz * 16, 16), 16), :]
        first, second = both[0:1, :], both[8:9, :]
        at = pl.ds(mult(zz * MAIN, 16), MAIN)
        mt[at, 0:TOK] = one((slot < CAP) & (group * CAP + slot == first))
        mt[at, TOK : 2 * TOK] = one((slot >= CAP) & (group * CAP + slot - CAP == second))
        xb[at, :] = one(group * CAP + slot % 4 + 6 == second)
        return 0

    lax.fori_loop(0, NZ, tables, 0)
    part = (iota((MAIN, TOK), 0) // 4) % 4

    def extra_pick(zz, q):
        base = xb[pl.ds(mult(zz * MAIN, 16), MAIN), :]
        return jnp.where(part == q, base.astype(F32), 0.0).astype(BF)

    def table(zz):
        return mt[pl.ds(mult(zz * MAIN, 16), MAIN), :]

    drain(tsend, t_r.at[0])
    gm[...] = dot(table(z), tok[...]).astype(BF)
    gx[...] = sum(
        dot(extra_pick(z, q), tok[TOK : 2 * TOK, q * XD : (q + 1) * XD]) for q in range(4)
    ).astype(BF)
    own_half = cols(c * HD, HD)
    for i, j in PLANE:
        p2, dev = plane(i, j)
        here = cot.at[pl.ds(mult(z * ROWS + p * 16, 16), 16), own_half]
        remote(rows(gm, p2 * 16, 16), here, cm_s.at[0], cm_r.at[0], dev).start()
        remote(rows(gx, p2 * 16, 16), rows(cxp, p * 16, 16), cx_s.at[0], cx_r.at[0], dev).start()
    local(
        rows(gm, p * 16, 16), cot.at[pl.ds(mult(z * ROWS + p * 16, 16), 16), own_half], cm_r.at[0]
    ).start()
    local(rows(gx, p * 16, 16), rows(cxp, p * 16, 16), cx_r.at[0]).start()

    def cot_block(zz, start, size):
        return cot.at[pl.ds(mult(zz * ROWS, 16), ROWS), cols(c * HD + start, size)]

    def to_sibling(zz):
        ref = cot_block(zz, 0, HD)
        remote(ref, ref, sib_s.at[zz], sib_r.at[zz], sib).start()

    drain(cxp, cx_r.at[0])
    place = (iota((EXT, MAIN), 0) // 4 == iota((EXT, MAIN), 1) // 16) & (
        iota((EXT, MAIN), 0) % 4 == iota((EXT, MAIN), 1) % 4
    )
    for q in range(4):
        unpack = one(place & ((iota((EXT, MAIN), 1) // 4) % 4 == q))
        cot[pl.ds(mult(z * ROWS + MAIN, 16), EXT), cols(c * HD + q * XD, XD)] = dot(
            unpack, cxp[...]
        ).astype(BF)
    drain(cot.at[pl.ds(mult(z * ROWS, 16), MAIN), own_half], cm_r.at[0])
    low, high = cot_block(z, 0, QD), cot_block(z, QD, QD)
    remote(low, low, ag_s.at[0], ag_r.at[0], up).start()
    remote(high, high, ag_s.at[1], ag_r.at[1], down).start()
    remote(high, high, ag_s.at[2], ag_r.at[2], up).start()
    remote(low, low, ag_s.at[3], ag_r.at[3], down).start()
    to_sibling(z)

    drain(xh, hz_r.at[0])
    sx[...] = sum(
        dot(extra_pick(zz, zz), xh[(2 * zz + 1) * TOK : (2 * zz + 2) * TOK, :]) for zz in range(NZ)
    ).astype(BF)

    def send_slots(src, dst_start, ref, ss, rs):
        for i, j in PLANE:
            p2, dev = plane(i, j)
            remote(src(p2), rows(ref, dst_start, 16), ss, rs, dev).start()
        local(src(p), rows(ref, dst_start, 16), rs).start()

    send_slots(lambda p2: rows(sx, p2 * 16, 16), p * 16, hxr, hm_s.at[4], hm_r.at[4])

    def order(k):
        return lax.rem(z + jnp.where(k == 2, 3, jnp.where(k == 3, 0, 2 - k)), 4)

    def pick_hidden(k, _):
        zz = order(k)
        at = pl.ds(mult(zz * MAIN, 16), MAIN)
        sm[at, :] = dot(table(zz), xh[at, :]).astype(BF)
        send_slots(
            lambda p2: rows(sm, zz * MAIN + p2 * 16, 16),
            zz * ROWS + p * 16,
            h,
            hm_s.at[zz],
            hm_r.at[zz],
        )
        return 0

    lax.fori_loop(0, NZ, pick_hidden, 0)

    drain(wv, w_sem.at[0])

    def slot_grads(zz):
        at = pl.ds(mult(zz * ROWS, 16), ROWS)
        hp[at, :] = dot_nt(cot[at, :], wv[...]).astype(BF)
        send_slots(
            lambda p2: rows(hp, zz * ROWS + p2 * 16, 16),
            zz * MAIN + p * 16,
            rm,
            ret_s.at[zz],
            ret_r.at[zz],
        )

    def other_half(zz):
        return cot.at[pl.ds(mult(zz * ROWS, 16), ROWS), cols(nc * HD, HD)]

    drain(other_half(z), sib_r.at[z])
    slot_grads(z)

    mine_out = pa.at[c]
    drain(hxr, hm_r.at[4])
    swap = one(
        (iota((MAIN, MAIN), 0) // 64 == (iota((MAIN, MAIN), 1) // 4) % 4)
        & ((iota((MAIN, MAIN), 0) // 4) % 16 == iota((MAIN, MAIN), 1) // 16)
        & (iota((MAIN, MAIN), 0) % 4 == iota((MAIN, MAIN), 1) % 4)
    )
    moved = dot(swap, hxr[...]).astype(BF)
    for zz in range(NZ):
        h[zz * ROWS + MAIN : (zz + 1) * ROWS, :] = moved[zz * EXT : (zz + 1) * EXT, :]

    def add_into(zz, start, size, ref):
        def step(i, _):
            at = pl.ds(mult(zz * ROWS + i * 32, 16), 32)
            where = cols(start, size)
            mine_out[at, where] = (
                mine_out[at, where].astype(F32) + ref(i)[...].astype(F32)
            ).astype(BF)
            return 0

        lax.fori_loop(0, ROWS // 32, step, 0)

    def add_cores(zz):
        drain(prcv.at[pl.ds(mult(zz * ROWS, 16), ROWS)], po_r.at[zz])
        add_into(zz, 0, HD, lambda i: prcv.at[pl.ds(mult(zz * ROWS + i * 32, 16), 32)])

    def out_block(zz, start):
        return mine_out.at[pl.ds(mult(zz * ROWS, 16), ROWS), pl.ds(start, QD)]

    def r2_half(n, start):
        return r2.at[n, :, pl.ds(start, QD)]

    def partials(k, _):
        zz = order(k)
        at = pl.ds(mult(zz * ROWS, 16), ROWS)

        @pl.when(k == 0)
        def _():
            drain(cot_block(zm, 0, QD), ag_r.at[0])
            ref = cot_block(zm, 0, QD)
            remote(ref, ref, agf_s.at[0], agf_r.at[0], up).start()
            drain(cot_block(zp, QD, QD), ag_r.at[1])
            ref2 = cot_block(zp, QD, QD)
            remote(ref2, ref2, agf_s.at[1], agf_r.at[1], down).start()

        drain(h.at[pl.ds(mult(zz * ROWS, 16), MAIN)], hm_r.at[zz])
        rows_in = h[at, :]

        def product(half):
            def tile(j, _):
                pa[half, at, cols(j * QD, QD)] = dot(
                    rows_in, wv[:, cols(half * HD + j * QD, QD)]
                ).astype(BF)
                return 0

            lax.fori_loop(0, 2, tile, 0)

        product(nc)
        remote(
            pa.at[nc, at], prcv.at[at], po_s.at[zz], po_r.at[zz], sib
        ).start()
        product(c)

        @pl.when(k == 1)
        def _():
            add_cores(zo)
            remote(out_block(zo, 0), r1.at[0], rs_s.at[0], rs_r.at[0], up).start()
            remote(out_block(zo, QD), r1.at[1], rs_s.at[1], rs_r.at[1], down).start()

        @pl.when(k == 2)
        def _():
            add_cores(zp)
            remote(out_block(zp, QD), r2_half(0, QD), rs_s.at[2], rs_r.at[2], up).start()
            drain(cot_block(zm, QD, QD), ag_r.at[2])
            to_sibling(zm)
            drain(cot_block(zp, 0, QD), ag_r.at[3])
            to_sibling(zp)

        @pl.when(k == 3)
        def _():
            add_cores(zm)
            remote(out_block(zm, 0), r2_half(1, 0), rs_s.at[3], rs_r.at[3], down).start()

        return 0

    lax.fori_loop(0, NZ, partials, 0)
    add_cores(z)

    def more_grads(k, _):
        zz = lax.rem(z + jnp.where(k == 0, 1, jnp.where(k == 1, 3, 2)), 4)

        @pl.when(k == 2)
        def _():
            drain(cot_block(zo, 0, QD), agf_r.at[0])
            drain(cot_block(zo, QD, QD), agf_r.at[1])
            to_sibling(zo)

        drain(other_half(zz), sib_r.at[zz])
        slot_grads(zz)
        return 0

    lax.fori_loop(0, 3, more_grads, 0)

    unswap = one(
        (iota((MAIN, MAIN), 1) // 64 == (iota((MAIN, MAIN), 0) // 4) % 4)
        & ((iota((MAIN, MAIN), 1) // 4) % 16 == iota((MAIN, MAIN), 0) // 16)
        & (iota((MAIN, MAIN), 1) % 4 == iota((MAIN, MAIN), 0) % 4)
    )
    hpx[...] = sum(
        dot(unswap[:, zz * EXT : (zz + 1) * EXT], hp[zz * ROWS + MAIN : (zz + 1) * ROWS, :])
        for zz in range(NZ)
    ).astype(BF)
    send_slots(lambda p2: rows(hpx, p2 * 16, 16), p * 16, rx, ret_s.at[4], ret_r.at[4])

    drain(r1.at[0], rs_r.at[0])
    add_into(zp, 0, QD, lambda i: r1.at[0, pl.ds(mult(i * 32, 16), 32)])
    remote(out_block(zp, 0), r2_half(0, 0), rs_s.at[4], rs_r.at[4], up).start()
    drain(r1.at[1], rs_r.at[1])
    add_into(zm, QD, QD, lambda i: r1.at[1, pl.ds(mult(i * 32, 16), 32)])
    remote(out_block(zm, QD), r2_half(1, QD), rs_s.at[5], rs_r.at[5], down).start()

    for zz in range(NZ):
        drain(pa.at[0, 0:ROWS], po_s.at[zz])

    def weight_tile(j):
        src = pa.at[nc, pl.ds(0, FB), cols(lax.rem(j, 4) * XD, XD)]
        return src, local(src, wg.at[:, cols(j * XD, XD)], wg_sem.at[lax.rem(j, 4)])

    def weight_grads(j, _):
        src, copy = weight_tile(j)

        @pl.when(j >= 4)
        def _():
            copy.wait()

        src[...] = dot_tn(h[...], cot[:, cols(j * XD, XD)]).astype(BF)
        copy.start()
        return 0

    lax.fori_loop(0, 8, weight_grads, 0)

    drain(rx, ret_r.at[4])

    def tokens_grad(zz, _):
        at = pl.ds(mult(zz * MAIN, 16), MAIN)
        drain(rm.at[at], ret_r.at[zz])
        grads = dot_tn(table(zz), rm[at, :])
        late = dot_tn(extra_pick(zz, zz), rx[...])
        xh[pl.ds(mult(zz * MAIN, 16), TOK), :] = grads[0:TOK, :].astype(BF)
        xh[pl.ds(mult(zz * MAIN + TOK, 16), TOK), :] = (grads[TOK:, :] + late).astype(BF)
        return 0

    lax.fori_loop(0, NZ, tokens_grad, 0)

    drain(r2_half(0, 0), rs_r.at[4])
    drain(r2_half(0, QD), rs_r.at[2])
    add_into(z, 0, HD, lambda i: r2.at[0, pl.ds(mult(i * 32, 16), 32)])
    drain(r2_half(1, 0), rs_r.at[3])
    drain(r2_half(1, QD), rs_r.at[5])
    add_into(z, 0, HD, lambda i: r2.at[1, pl.ds(mult(i * 32, 16), 32)])
    back = (iota((MAIN, EXT), 1) // 4 == iota((MAIN, EXT), 0) // 16) & (
        iota((MAIN, EXT), 1) % 4 == iota((MAIN, EXT), 0) % 4
    )
    tail = mine_out[pl.ds(mult(z * ROWS + MAIN, 16), EXT), :]
    ex[...] = sum(
        dot(one(back & ((iota((MAIN, EXT), 0) // 4) % 4 == q)), tail[:, q * XD : (q + 1) * XD])
        for q in range(4)
    ).astype(BF)
    send_slots(
        lambda p2: mine_out.at[pl.ds(mult(z * ROWS + p2 * 16, 16), 16)],
        p * 16,
        em,
        eo_s.at[0],
        eo_r.at[0],
    )
    send_slots(lambda p2: rows(ex, p2 * 16, 16), p * 16, exr, eo_s.at[1], eo_r.at[1])

    def return_grads(piece, _):
        for dc, dz in COLUMN:
            c2, z2, dev = column(dc, dz)
            src = rows(xh, (z2 * 2 + c2) * TOK + piece * 32, 32)
            dst = hg.at[pl.ds(mult(piece * 32, 16), 32), cols(blk * FB, FB)]
            remote(src, dst, hg_s.at[0], hg_r.at[0], dev).start()
        return 0

    lax.fori_loop(0, 4, return_grads, 0)
    local(rows(xh, (z * 2 + c) * TOK, TOK), hg.at[:, cols(blk * FB, FB)], hg_r.at[0]).start()

    drain(em, eo_r.at[0])
    drain(exr, eo_r.at[1])
    kk[...] = dot_tn(table(z), em[...]).astype(BF)
    for q in range(4):
        at = slice(q * XD, (q + 1) * XD)
        kk[TOK : 2 * TOK, at] = (
            kk[TOK : 2 * TOK, at].astype(F32) + dot_tn(extra_pick(z, q), exr[...])
        ).astype(BF)
    remote(rows(kk, nc * TOK, TOK), kr, k_s.at[0], k_r.at[0], sib).start()
    picked = kk[pl.ds(mult(c * TOK, 16), TOK), :].astype(F32)
    total = jnp.sum(og[:, cols(c * HD, HD)].astype(F32) * picked, axis=1, keepdims=True)
    mixed[:, cols(c * HD, HD)] = (gate * picked).astype(BF)
    drain(kr, k_r.at[0])
    picked2 = kr[...].astype(F32)
    total += jnp.sum(og[:, cols(nc * HD, HD)].astype(F32) * picked2, axis=1, keepdims=True)
    mixed[:, cols(nc * HD, HD)] = (gate * picked2).astype(BF)
    gg[...] = jnp.sum(jnp.where(eye, total, 0.0), axis=0, keepdims=True)

    drain(hg, hg_r.at[0])
    for j in range(4):
        weight_tile(j)[1].wait()
    drain(rows(posv, 0, 56, 8), pos_s.at[0])
    drain(xh.at[pl.ds(0, 7 * TOK)], hz_s.at[0])
    drain(xh.at[pl.ds(0, 7 * TOK)], hg_s.at[0])
    drain(tsend, t_s.at[0])
    drain(gm.at[pl.ds(0, 240)], cm_s.at[0])
    drain(gx.at[pl.ds(0, 240)], cx_s.at[0])
    for n in range(5):
        drain(hp.at[pl.ds(0, 240)], hm_s.at[n])
        drain(hp.at[pl.ds(0, 240)], ret_s.at[n])
    for n in range(4):
        drain(r1.at[0], ag_s.at[n])
        drain(r2.at[0], sib_s.at[n])
    for n in range(2):
        drain(r1.at[0], agf_s.at[n])
    for n in range(6):
        drain(r1.at[0], rs_s.at[n])
    drain(em.at[pl.ds(0, 240)], eo_s.at[0])
    drain(exr.at[pl.ds(0, 240)], eo_s.at[1])
    drain(kr, k_s.at[0])


def layer(hidden_in, weights, gates, group_ids, slot_ids, out_grad):
    position = jnp.broadcast_to((group_ids * CAP + slot_ids)[None, :], (8, TOK))
    vmem = pl.BlockSpec(memory_space=pltpu.VMEM)
    anywhere = pl.BlockSpec(memory_space=pl.ANY)
    sem = pltpu.SemaphoreType.DMA

    def buf(*shape):
        return pltpu.VMEM(shape, BF)

    mixed, hidden_grad, weight_grad, gate_grad = pl.pallas_call(
        kernel,
        out_shape=(
            jax.ShapeDtypeStruct((TOK, D), BF),
            jax.ShapeDtypeStruct((TOK, FF), BF),
            jax.ShapeDtypeStruct((FB, D), BF),
            jax.ShapeDtypeStruct((1, TOK), F32),
        ),
        in_specs=[anywhere, anywhere, vmem, vmem, anywhere],
        out_specs=(vmem, anywhere, anywhere, vmem),
        scratch_shapes=[
            buf(FB, D),
            buf(NZ * ROWS, FB),
            buf(MAIN, FB),
            buf(NZ * ROWS, D),
            buf(MAIN, XD),
            buf(8 * TOK, FB),
            buf(NZ * MAIN, FB),
            buf(MAIN, FB),
            buf(2 * TOK, HD),
            buf(TOK, HD),
            buf(MAIN, HD),
            buf(MAIN, XD),
            buf(2, NZ * ROWS, HD),
            buf(NZ * ROWS, HD),
            buf(2, ROWS, QD),
            buf(2, ROWS, HD),
            buf(MAIN, XD),
            buf(MAIN, HD),
            buf(MAIN, XD),
            buf(NZ * ROWS, FB),
            buf(MAIN, FB),
            buf(NZ * MAIN, FB),
            buf(MAIN, FB),
            buf(2 * TOK, HD),
            buf(TOK, HD),
            buf(TOK, D),
            buf(NZ * MAIN, 2 * TOK),
            buf(NZ * MAIN, TOK),
            pltpu.VMEM((8 * 8, TOK), jnp.int32),
            sem((1,)), sem((1,)),
            sem((1,)), sem((1,)),
            sem((1,)), sem((1,)),
            sem((1,)), sem((1,)),
            sem((1,)), sem((1,)),
            sem((1,)), sem((1,)),
            sem((5,)), sem((5,)),
            sem((4,)), sem((4,)),
            sem((2,)), sem((2,)),
            sem((4,)), sem((4,)),
            sem((4,)), sem((4,)),
            sem((6,)), sem((6,)),
            sem((5,)), sem((5,)),
            sem((2,)), sem((2,)),
            sem((1,)), sem((1,)),
            sem((1,)), sem((1,)),
            sem((4,)),
        ],
        compiler_params=pltpu.CompilerParams(
            collective_id=0, has_side_effects=True, vmem_limit_bytes=64 * 1024 * 1024 - 65536
        ),
        cost_estimate=pl.CostEstimate(
            flops=6 * NZ * ROWS * FB * D, bytes_accessed=20_000_000, transcendentals=0
        ),
        name="experts",
    )(hidden_in, weights, gates.reshape(1, TOK), position, out_grad)
    return mixed, hidden_grad, weight_grad, gate_grad.reshape(TOK)


def solution(mesh):
    wide, flat = P(("grp", "exp"), None), P(("grp", "exp"))
    return jax.shard_map(
        layer,
        mesh=mesh,
        in_specs=(wide, wide, flat, flat, flat, wide),
        out_specs=(wide, wide, wide, flat),
        check_vma=False,
    )
```

time: 342 us -> 158 us (0.46)
  Pallas kernels: 0 us -> 143 us
  blocking collectives: 104 us -> 0 us
  waiting for transfers between devices: 59.7 us -> 0 us
  matrix products: 57.6 us -> 0 us
  local copies, waits for them, and re-layouts: 68 us -> 13.3 us
  starting transfers between devices: 19.8 us -> 0 us
  other arithmetic: 17.6 us -> 0.68 us
  between operations: 14.3 us -> 0.64 us
    pallas_call x0 -> x1, Pallas kernels: none -> 143 us  [layer(): pl.pallas_call(kernel, out_shape=(jax.ShapeDtypeStruct((TOK, D), BF), jax...]
    all_to_all x3 -> x0, blocking collectives: 104 us -> none  [the longest x1 36.5 us: local(): lax.all_to_all(split_cot, 'grp', split_axis=0, concat_axis=0, tiled=True)]
    dot_general x8 -> x0, matrix products: 57.6 us -> none  [the longest x1 17 us: local(): jnp.dot(rows_in, weights, preferred_element_type=jnp.float32)]
    reshape x13 -> x0, local copies, waits for them, and re-layouts: 45.7 us -> none  [the longest x1 9.94 us: local(): lax.all_gather(received, 'exp', axis=0, tiled=True).reshape(-1, half_d)]
    reduce_scatter x1 -> x0, waiting for transfers between devices: 29.4 us -> none  [local(): lax.psum_scatter(lax.optimization_barrier(partial_value.astype(jnp.bfloat...]
    all_to_all x3 -> x0, waiting for transfers between devices: 21.6 us -> none  [the longest x1 21.6 us: local(): lax.all_to_all(lax.all_to_all(grad_blocks, 'grp', split_axis=1, concat_ax...]
    all_to_all x3 -> x0, starting transfers between devices: 17.6 us -> none  [the longest x1 7.69 us: local(): lax.all_to_all(expert_half, 'grp', split_axis=0, concat_axis=0, tiled=True)]
    unnamed x11 -> x6, local copies, waits for them, and re-layouts: 2.89 us -> 12.7 us
  transfers between devices with their start and end apart: 7 -> 0, of which waited for: 3 -> 0; matrix products, arithmetic and copies ran while one was open for 38% -> 0% of each run, Pallas kernels for 0% -> 0%
where the time goes in v1:
time: 158 us
  Pallas kernels  143 us (91%)
  local copies, waits for them, and re-layouts  13.3 us (8%)
    pallas_call x1, Pallas kernels, layer(): pl.pallas_call(kernel, out_shape=(jax.ShapeDtypeStruct((TOK, D), BF), jax...  143 us
    unnamed x6, local copies, waits for them, and re-layouts  12.7 us

profile of v1, /device:TPU:1, one launch (start us, length us, event | category | flops | bytes accessed | tf_op | source)
XLA Modules:
  0.0 157.5 jit_solution(7754065393169707245)
XLA Ops:
  0.6 0.7 multiply_add_fusion
  1.3 0.6 broadcast_in_dim.2.pos
  1.9 142.9 %experts.1 = (bf16[128,4096]{1,0:T(8,128)(2,1)}, bf16[128,7168]{1,0:T(8,128)(2,1)}, bf16[896,4096]{1,0:T(8,128)(2,1)}, f32[1,128]{1,0:T(1,128)}) custom-call(bf16[128,7168]{1,0:T(8,128)(2,1)} %hid.1, bf16[896,4096]{1,0:T(8,128)(2,1)} %w_hbm.1, f32[1,128]{1,0:T(1,128)} %bitcast.2, s32[8,128]{1,0:T(8,128)} %broadcast_in_dim.2.pos, bf16[128,4096]{1,0:T(8,128)(2,1)} %og_hbm.1), custom_call_target="tpu_custom_call" | custom-call | flops 28185722880 | bytes 20000000 | tf_op jit(solution)/shard_map/experts/pallas_call | solution.py:488
  144.8 2.3 %copy.14 = bf16[128,4096]{1,0:T(8,128)(2,1)} copy(bf16[128,4096]{1,0:T(8,128)(2,1)} %get-tuple-element.16) | data formatting | bytes 2097152
  147.1 2.8 %copy.15 = bf16[128,7168]{1,0:T(8,128)(2,1)} copy(bf16[128,7168]{1,0:T(8,128)(2,1)} %get-tuple-element.17) | data formatting | bytes 3670016
  149.9 0.0 copy-start
  149.9 7.1 %copy.16 = bf16[896,4096]{1,0:T(8,128)(2,1)} copy(bf16[896,4096]{1,0:T(8,128)(2,1)} %get-tuple-element.18) | data formatting | bytes 14680064
  157.0 0.0 copy-done
  157.0 0.5 copy.17
Async XLA Ops:
  149.9 7.1 %copy-start = (f32[1,128]{1,0:T(1,128)S(1)}, f32[1,128]{1,0:T(1,128)}, u32[]{:S(2)}) copy-start(f32[1,128]{1,0:T(1,128)} %get-tuple-element.11) | copy-start | bytes 1540

commit v2 on v1

--- a/solution.py
+++ b/solution.py
@@ -52,11 +52,11 @@
 
 
 def kernel(
-    hid, w_hbm, gates, pos, og_hbm,
-    mixed, hg, wg, gg,
-    wv, h, hxr, cot, cxp, xh, sm, sx, tok, tsend, gm, gx, pa, prcv, r1, r2, ex, em, exr, hp, hpx, rm, rx, kk, kr, og,
+    hid, w_hbm, gates, group_ids, slot_ids, og_hbm,
+    picked, hg, wg,
+    wv, h, hxr, cot, cxp, xh, sm, sx, tok, tsend, gm, gx, pa, prcv, r1, r2, ex, em, exr, hp, hpx, rm, rx, kk, og,
     mt, xb, posv,
-    pos_s, pos_r, hz_s, hz_r, w_sem, og_sem, t_s, t_r, cm_s, cm_r, cx_s, cx_r, hm_s, hm_r,
+    pos_s, pos_r, hz_s, hz_r, w_sem, og_sem, st_sem, t_s, t_r, cm_s, cm_r, cx_s, cx_r, hm_s, hm_r,
     ag_s, ag_r, agf_s, agf_r, sib_s, sib_r, po_s, po_r, rs_s, rs_r, ret_s, ret_r, eo_s, eo_r, k_s, k_r, hg_s, hg_r, wg_sem,
 ):
     g = lax.axis_index("grp")
@@ -100,37 +100,40 @@
     def cols(start, size):
         return pl.ds(mult(start, 128), size)
 
-    local(og_hbm, og, og_sem.at[0]).start()
-    local(w_hbm, wv, w_sem.at[0]).start()
-    posv[pl.ds(mult((z * 2 + c) * 8, 8), 8), :] = pos[...]
-
     barrier = pltpu.get_barrier_semaphore()
     for dc, dz in COLUMN:
         pl.semaphore_signal(barrier, inc=1, device_id=column(dc, dz)[2], device_id_type=MESH)
     for i, j in PLANE:
         pl.semaphore_signal(barrier, inc=1, device_id=plane(i, j)[1], device_id_type=MESH)
-    pl.semaphore_wait(barrier, len(COLUMN) + len(PLANE))
-
-    mine = rows(posv, (z * 2 + c) * 8, 8, 8)
-    for dc, dz in COLUMN:
-        remote(mine, mine, pos_s.at[0], pos_r.at[0], column(dc, dz)[2]).start()
-
-    def send_hidden(piece, _):
-        for dc, dz in COLUMN:
-            c2, z2, dev = column(dc, dz)
-            src = hid.at[pl.ds(mult(piece * 32, 16), 32), cols((c2 * 4 + z2) * FB, FB)]
-            dst = rows(xh, (z * 2 + c) * TOK + piece * 32, 32)
-            remote(src, dst, hz_s.at[0], hz_r.at[0], dev).start()
-        return 0
-
-    lax.fori_loop(0, 4, send_hidden, 0)
-    local(hid.at[:, cols(blk * FB, FB)], rows(xh, (z * 2 + c) * TOK, TOK), hz_r.at[0]).start()
-
+
+    local(og_hbm, og, og_sem.at[0]).start()
+    for k in range(8):
+        local(hid.at[:, pl.ds(k * FB, FB)], hp.at[pl.ds(k * TOK, TOK)], st_sem.at[0]).start()
+    local(w_hbm, wv, w_sem.at[0]).start()
+    position = group_ids[...] * CAP + slot_ids[...]
+    posv[pl.ds(mult((z * 2 + c) * 8, 8), 8), :] = jnp.broadcast_to(position, (8, TOK))
     eye = iota((TOK, TOK), 0) == iota((TOK, TOK), 1)
     gate = jnp.sum(jnp.where(eye, gates[...], 0.0), axis=1, keepdims=True)
     drain(og, og_sem.at[0])
     tsend[...] = (gate * og[:, cols(nc * HD, HD)].astype(F32)).astype(BF)
+    drain(hp.at[pl.ds(0, 8 * TOK)], st_sem.at[0])
+    pl.semaphore_wait(barrier, len(COLUMN) + len(PLANE))
+
     remote(tsend, rows(tok, c * TOK, TOK), t_s.at[0], t_r.at[0], sib).start()
+    mine = rows(posv, (z * 2 + c) * 8, 8, 8)
+    for dc, dz in COLUMN:
+        remote(mine, mine, pos_s.at[0], pos_r.at[0], column(dc, dz)[2]).start()
+
+    def send_hidden(piece, _):
+        for dc, dz in COLUMN:
+            c2, z2, dev = column(dc, dz)
+            src = rows(hp, (c2 * 4 + z2) * TOK + piece * 32, 32)
+            dst = rows(xh, (z * 2 + c) * TOK + piece * 32, 32)
+            remote(src, dst, hz_s.at[0], hz_r.at[0], dev).start()
+        return 0
+
+    lax.fori_loop(0, 4, send_hidden, 0)
+    local(rows(hp, blk * TOK, TOK), rows(xh, (z * 2 + c) * TOK, TOK), hz_r.at[0]).start()
     tok[pl.ds(mult(c * TOK, 16), TOK), :] = (gate * og[:, cols(c * HD, HD)].astype(F32)).astype(BF)
 
     drain(rows(posv, 0, 56, 8), pos_r.at[0])
@@ -156,21 +159,28 @@
     def table(zz):
         return mt[pl.ds(mult(zz * MAIN, 16), MAIN), :]
 
+    def half(ref, start, size, n):
+        return ref.at[pl.ds(mult(start, 16), size), pl.ds(n * QD, QD)]
+
+    def cot_half(start, size, n):
+        return cot.at[pl.ds(mult(start, 16), size), cols(c * HD + n * QD, QD)]
+
+    def send_slots(src, dst, ss, rs):
+        for i, j in PLANE:
+            p2, dev = plane(i, j)
+            remote(src(p2), dst, ss, rs, dev).start()
+        local(src(p), dst, rs).start()
+
     drain(tsend, t_r.at[0])
-    gm[...] = dot(table(z), tok[...]).astype(BF)
     gx[...] = sum(
         dot(extra_pick(z, q), tok[TOK : 2 * TOK, q * XD : (q + 1) * XD]) for q in range(4)
     ).astype(BF)
-    own_half = cols(c * HD, HD)
-    for i, j in PLANE:
-        p2, dev = plane(i, j)
-        here = cot.at[pl.ds(mult(z * ROWS + p * 16, 16), 16), own_half]
-        remote(rows(gm, p2 * 16, 16), here, cm_s.at[0], cm_r.at[0], dev).start()
-        remote(rows(gx, p2 * 16, 16), rows(cxp, p * 16, 16), cx_s.at[0], cx_r.at[0], dev).start()
-    local(
-        rows(gm, p * 16, 16), cot.at[pl.ds(mult(z * ROWS + p * 16, 16), 16), own_half], cm_r.at[0]
-    ).start()
-    local(rows(gx, p * 16, 16), rows(cxp, p * 16, 16), cx_r.at[0]).start()
+    send_slots(lambda p2: rows(gx, p2 * 16, 16), rows(cxp, p * 16, 16), cx_s.at[0], cx_r.at[0])
+    for n in range(2):
+        gm[:, n * QD : (n + 1) * QD] = dot(table(z), tok[:, n * QD : (n + 1) * QD]).astype(BF)
+        send_slots(
+            lambda p2: half(gm, p2 * 16, 16, n), cot_half(z * ROWS + p * 16, 16, n), cm_s.at[n], cm_r.at[n]
+        )
 
     def cot_block(zz, start, size):
         return cot.at[pl.ds(mult(zz * ROWS, 16), ROWS), cols(c * HD + start, size)]
@@ -188,12 +198,11 @@
         cot[pl.ds(mult(z * ROWS + MAIN, 16), EXT), cols(c * HD + q * XD, XD)] = dot(
             unpack, cxp[...]
         ).astype(BF)
-    drain(cot.at[pl.ds(mult(z * ROWS, 16), MAIN), own_half], cm_r.at[0])
-    low, high = cot_block(z, 0, QD), cot_block(z, QD, QD)
-    remote(low, low, ag_s.at[0], ag_r.at[0], up).start()
-    remote(high, high, ag_s.at[1], ag_r.at[1], down).start()
-    remote(high, high, ag_s.at[2], ag_r.at[2], up).start()
-    remote(low, low, ag_s.at[3], ag_r.at[3], down).start()
+    for n in range(2):
+        drain(cot_half(z * ROWS, MAIN, n), cm_r.at[n])
+        ref = cot_block(z, n * QD, QD)
+        remote(ref, ref, ag_s.at[2 * n], ag_r.at[2 * n], up).start()
+        remote(ref, ref, ag_s.at[2 * n + 1], ag_r.at[2 * n + 1], down).start()
     to_sibling(z)
 
     drain(xh, hz_r.at[0])
@@ -201,13 +210,7 @@
         dot(extra_pick(zz, zz), xh[(2 * zz + 1) * TOK : (2 * zz + 2) * TOK, :]) for zz in range(NZ)
     ).astype(BF)
 
-    def send_slots(src, dst_start, ref, ss, rs):
-        for i, j in PLANE:
-            p2, dev = plane(i, j)
-            remote(src(p2), rows(ref, dst_start, 16), ss, rs, dev).start()
-        local(src(p), rows(ref, dst_start, 16), rs).start()
-
-    send_slots(lambda p2: rows(sx, p2 * 16, 16), p * 16, hxr, hm_s.at[4], hm_r.at[4])
+    send_slots(lambda p2: rows(sx, p2 * 16, 16), rows(hxr, p * 16, 16), hm_s.at[4], hm_r.at[4])
 
     def order(k):
         return lax.rem(z + jnp.where(k == 2, 3, jnp.where(k == 3, 0, 2 - k)), 4)
@@ -218,8 +221,7 @@
         sm[at, :] = dot(table(zz), xh[at, :]).astype(BF)
         send_slots(
             lambda p2: rows(sm, zz * MAIN + p2 * 16, 16),
-            zz * ROWS + p * 16,
-            h,
+            rows(h, zz * ROWS + p * 16, 16),
             hm_s.at[zz],
             hm_r.at[zz],
         )
@@ -228,14 +230,15 @@
     lax.fori_loop(0, NZ, pick_hidden, 0)
 
     drain(wv, w_sem.at[0])
+
+    drain(hp.at[pl.ds(0, 7 * TOK)], hz_s.at[0])
 
     def slot_grads(zz):
         at = pl.ds(mult(zz * ROWS, 16), ROWS)
         hp[at, :] = dot_nt(cot[at, :], wv[...]).astype(BF)
         send_slots(
             lambda p2: rows(hp, zz * ROWS + p2 * 16, 16),
-            zz * MAIN + p * 16,
-            rm,
+            rows(rm, zz * MAIN + p * 16, 16),
             ret_s.at[zz],
             ret_r.at[zz],
         )
@@ -287,7 +290,7 @@
             drain(cot_block(zm, 0, QD), ag_r.at[0])
             ref = cot_block(zm, 0, QD)
             remote(ref, ref, agf_s.at[0], agf_r.at[0], up).start()
-            drain(cot_block(zp, QD, QD), ag_r.at[1])
+            drain(cot_block(zp, QD, QD), ag_r.at[3])
             ref2 = cot_block(zp, QD, QD)
             remote(ref2, ref2, agf_s.at[1], agf_r.at[1], down).start()
 
@@ -321,7 +324,7 @@
             remote(out_block(zp, QD), r2_half(0, QD), rs_s.at[2], rs_r.at[2], up).start()
             drain(cot_block(zm, QD, QD), ag_r.at[2])
             to_sibling(zm)
-            drain(cot_block(zp, 0, QD), ag_r.at[3])
+            drain(cot_block(zp, 0, QD), ag_r.at[1])
             to_sibling(zp)
 
         @pl.when(k == 3)
@@ -358,7 +361,7 @@
         dot(unswap[:, zz * EXT : (zz + 1) * EXT], hp[zz * ROWS + MAIN : (zz + 1) * ROWS, :])
         for zz in range(NZ)
     ).astype(BF)
-    send_slots(lambda p2: rows(hpx, p2 * 16, 16), p * 16, rx, ret_s.at[4], ret_r.at[4])
+    send_slots(lambda p2: rows(hpx, p2 * 16, 16), rows(rx, p * 16, 16), ret_s.at[4], ret_r.at[4])
 
     drain(r1.at[0], rs_r.at[0])
     add_into(zp, 0, QD, lambda i: r1.at[0, pl.ds(mult(i * 32, 16), 32)])
@@ -402,10 +405,25 @@
 
     drain(r2_half(0, 0), rs_r.at[4])
     drain(r2_half(0, QD), rs_r.at[2])
-    add_into(z, 0, HD, lambda i: r2.at[0, pl.ds(mult(i * 32, 16), 32)])
     drain(r2_half(1, 0), rs_r.at[3])
     drain(r2_half(1, QD), rs_r.at[5])
-    add_into(z, 0, HD, lambda i: r2.at[1, pl.ds(mult(i * 32, 16), 32)])
+
+    def last_sum(first, count, start, size):
+        def step(i, _):
+            from_row = first + i * 32
+            at = pl.ds(mult(z * ROWS + from_row, 16), 32)
+            there = pl.ds(mult(from_row, 16), 32)
+            where = pl.ds(start, size)
+            mine_out[at, where] = (
+                mine_out[at, where].astype(F32)
+                + r2[0, there, where].astype(F32)
+                + r2[1, there, where].astype(F32)
+            ).astype(BF)
+            return 0
+
+        lax.fori_loop(0, count // 32, step, 0)
+
+    last_sum(MAIN, EXT, 0, HD)
     back = (iota((MAIN, EXT), 1) // 4 == iota((MAIN, EXT), 0) // 16) & (
         iota((MAIN, EXT), 1) % 4 == iota((MAIN, EXT), 0) % 4
     )
@@ -414,14 +432,15 @@
         dot(one(back & ((iota((MAIN, EXT), 0) // 4) % 4 == q)), tail[:, q * XD : (q + 1) * XD])
         for q in range(4)
     ).astype(BF)
-    send_slots(
-        lambda p2: mine_out.at[pl.ds(mult(z * ROWS + p2 * 16, 16), 16)],
-        p * 16,
-        em,
-        eo_s.at[0],
-        eo_r.at[0],
-    )
-    send_slots(lambda p2: rows(ex, p2 * 16, 16), p * 16, exr, eo_s.at[1], eo_r.at[1])
+    send_slots(lambda p2: rows(ex, p2 * 16, 16), rows(exr, p * 16, 16), eo_s.at[2], eo_r.at[2])
+    for n in range(2):
+        last_sum(0, MAIN, n * QD, QD)
+        send_slots(
+            lambda p2: half(mine_out, z * ROWS + p2 * 16, 16, n),
+            half(em, p * 16, 16, n),
+            eo_s.at[n],
+            eo_r.at[n],
+        )
 
     def return_grads(piece, _):
         for dc, dz in COLUMN:
@@ -434,32 +453,30 @@
     lax.fori_loop(0, 4, return_grads, 0)
     local(rows(xh, (z * 2 + c) * TOK, TOK), hg.at[:, cols(blk * FB, FB)], hg_r.at[0]).start()
 
-    drain(em, eo_r.at[0])
-    drain(exr, eo_r.at[1])
-    kk[...] = dot_tn(table(z), em[...]).astype(BF)
-    for q in range(4):
-        at = slice(q * XD, (q + 1) * XD)
-        kk[TOK : 2 * TOK, at] = (
-            kk[TOK : 2 * TOK, at].astype(F32) + dot_tn(extra_pick(z, q), exr[...])
-        ).astype(BF)
-    remote(rows(kk, nc * TOK, TOK), kr, k_s.at[0], k_r.at[0], sib).start()
-    picked = kk[pl.ds(mult(c * TOK, 16), TOK), :].astype(F32)
-    total = jnp.sum(og[:, cols(c * HD, HD)].astype(F32) * picked, axis=1, keepdims=True)
-    mixed[:, cols(c * HD, HD)] = (gate * picked).astype(BF)
-    drain(kr, k_r.at[0])
-    picked2 = kr[...].astype(F32)
-    total += jnp.sum(og[:, cols(nc * HD, HD)].astype(F32) * picked2, axis=1, keepdims=True)
-    mixed[:, cols(nc * HD, HD)] = (gate * picked2).astype(BF)
-    gg[...] = jnp.sum(jnp.where(eye, total, 0.0), axis=0, keepdims=True)
-
+    drain(exr, eo_r.at[2])
+    for n in range(2):
+        drain(half(em, 0, MAIN, n), eo_r.at[n])
+        rows_out = dot_tn(table(z), em[:, n * QD : (n + 1) * QD])
+        late = jnp.concatenate([dot_tn(extra_pick(z, 2 * n + q), exr[...]) for q in range(2)], axis=1)
+        kk[0:TOK, n * QD : (n + 1) * QD] = rows_out[0:TOK, :].astype(BF)
+        kk[TOK : 2 * TOK, n * QD : (n + 1) * QD] = (rows_out[TOK:, :] + late).astype(BF)
+        there = picked.at[:, cols(c * HD + n * QD, QD)]
+        remote(half(kk, nc * TOK, TOK, n), there, k_s.at[n], k_r.at[n], sib).start()
+        local(half(kk, c * TOK, TOK, n), there, k_s.at[2 + n]).start()
+
+    for n in range(2):
+        drain(picked.at[:, cols(nc * HD + n * QD, QD)], k_r.at[n])
+        drain(half(kk, 0, TOK, n), k_s.at[n])
+        drain(half(kk, 0, TOK, n), k_s.at[2 + n])
     drain(hg, hg_r.at[0])
     for j in range(4):
         weight_tile(j)[1].wait()
     drain(rows(posv, 0, 56, 8), pos_s.at[0])
-    drain(xh.at[pl.ds(0, 7 * TOK)], hz_s.at[0])
     drain(xh.at[pl.ds(0, 7 * TOK)], hg_s.at[0])
     drain(tsend, t_s.at[0])
-    drain(gm.at[pl.ds(0, 240)], cm_s.at[0])
+    for n in range(2):
+        drain(half(gm, 0, 240, n), cm_s.at[n])
+        drain(half(em, 0, 240, n), eo_s.at[n])
     drain(gx.at[pl.ds(0, 240)], cx_s.at[0])
     for n in range(5):
         drain(hp.at[pl.ds(0, 240)], hm_s.at[n])
@@ -471,13 +488,51 @@
         drain(r1.at[0], agf_s.at[n])
     for n in range(6):
         drain(r1.at[0], rs_s.at[n])
-    drain(em.at[pl.ds(0, 240)], eo_s.at[0])
-    drain(exr.at[pl.ds(0, 240)], eo_s.at[1])
-    drain(kr, k_s.at[0])
+    drain(exr.at[pl.ds(0, 240)], eo_s.at[2])
+
+
+PIECES = 8
+
+
+def finish(
+    picked_hbm, gates, og_hbm, hg_in, wg_in, mixed, hg, wg, gg, picked, og, out, hbuf, wbuf, in_sem, out_sem
+):
+    copies = []
+    for k in range(PIECES):
+        at = pl.ds(k * (FB // PIECES), FB // PIECES)
+        copies.append((wg_in.at[at], wbuf.at[at], wg.at[at]))
+    for k in range(2):
+        at = pl.ds(k * (TOK // 2), TOK // 2)
+        copies.append((hg_in.at[at], hbuf.at[at], hg.at[at]))
+    loads = [pltpu.make_async_copy(a, b, in_sem.at[k]) for k, (a, b, _) in enumerate(copies)]
+    stores = [pltpu.make_async_copy(b, a, out_sem.at[k]) for k, (_, b, a) in enumerate(copies)]
+    rows_in = [
+        pltpu.make_async_copy(picked_hbm, picked, in_sem.at[PIECES + 2]),
+        pltpu.make_async_copy(og_hbm, og, in_sem.at[PIECES + 3]),
+    ]
+    for copy in rows_in + loads:
+        copy.start()
+    eye = iota((TOK, TOK), 0) == iota((TOK, TOK), 1)
+    gate = jnp.sum(jnp.where(eye, gates[...], 0.0), axis=1, keepdims=True)
+    for copy in rows_in:
+        copy.wait()
+    rows = picked[...].astype(F32)
+    out[...] = (gate * rows).astype(BF)
+    store = pltpu.make_async_copy(out, mixed, out_sem.at[PIECES + 2])
+    store.start()
+    for load, copy in zip(loads[:4], stores):
+        load.wait()
+        copy.start()
+    total = jnp.sum(og[...].astype(F32) * rows, axis=1, keepdims=True)
+    gg[...] = jnp.sum(jnp.where(eye, total, 0.0), axis=0, keepdims=True)
+    for load, copy in zip(loads[4:], stores[4:]):
+        load.wait()
+        copy.start()
+    for copy in stores + [store]:
+        copy.wait()
 
 
 def layer(hidden_in, weights, gates, group_ids, slot_ids, out_grad):
-    position = jnp.broadcast_to((group_ids * CAP + slot_ids)[None, :], (8, TOK))
     vmem = pl.BlockSpec(memory_space=pltpu.VMEM)
     anywhere = pl.BlockSpec(memory_space=pl.ANY)
     sem = pltpu.SemaphoreType.DMA
@@ -485,16 +540,16 @@
     def buf(*shape):
         return pltpu.VMEM(shape, BF)
 
-    mixed, hidden_grad, weight_grad, gate_grad = pl.pallas_call(
+    gate_row = gates.reshape(1, TOK)
+    picked, hidden_grad, weight_grad = pl.pallas_call(
         kernel,
         out_shape=(
             jax.ShapeDtypeStruct((TOK, D), BF),
             jax.ShapeDtypeStruct((TOK, FF), BF),
             jax.ShapeDtypeStruct((FB, D), BF),
-            jax.ShapeDtypeStruct((1, TOK), F32),
         ),
-        in_specs=[anywhere, anywhere, vmem, vmem, anywhere],
-        out_specs=(vmem, anywhere, anywhere, vmem),
+        in_specs=[anywhere, anywhere, vmem, vmem, vmem, anywhere],
+        out_specs=(anywhere, anywhere, anywhere),
         scratch_shapes=[
             buf(FB, D),
             buf(NZ * ROWS, FB),
@@ -520,16 +575,15 @@
             buf(NZ * MAIN, FB),
             buf(MAIN, FB),
             buf(2 * TOK, HD),
-            buf(TOK, HD),
             buf(TOK, D),
             buf(NZ * MAIN, 2 * TOK),
             buf(NZ * MAIN, TOK),
             pltpu.VMEM((8 * 8, TOK), jnp.int32),
             sem((1,)), sem((1,)),
             sem((1,)), sem((1,)),
+            sem((1,)), sem((1,)), sem((1,)),
             sem((1,)), sem((1,)),
-            sem((1,)), sem((1,)),
-            sem((1,)), sem((1,)),
+            sem((2,)), sem((2,)),
             sem((1,)), sem((1,)),
             sem((5,)), sem((5,)),
             sem((4,)), sem((4,)),
@@ -538,8 +592,8 @@
             sem((4,)), sem((4,)),
             sem((6,)), sem((6,)),
             sem((5,)), sem((5,)),
-            sem((2,)), sem((2,)),
-            sem((1,)), sem((1,)),
+            sem((3,)), sem((3,)),
+            sem((4,)), sem((2,)),
             sem((1,)), sem((1,)),
             sem((4,)),
         ],
@@ -550,7 +604,25 @@
             flops=6 * NZ * ROWS * FB * D, bytes_accessed=20_000_000, transcendentals=0
         ),
         name="experts",
-    )(hidden_in, weights, gates.reshape(1, TOK), position, out_grad)
+    )(hidden_in, weights, gate_row, group_ids.reshape(1, TOK), slot_ids.reshape(1, TOK), out_grad)
+
+    mixed, hidden_grad, weight_grad, gate_grad = pl.pallas_call(
+        finish,
+        out_shape=(
+            jax.ShapeDtypeStruct((TOK, D), BF),
+            jax.ShapeDtypeStruct((TOK, FF), BF),
+            jax.ShapeDtypeStruct((FB, D), BF),
+            jax.ShapeDtypeStruct((1, TOK), F32),
+        ),
+        in_specs=[anywhere, vmem, anywhere, anywhere, anywhere],
+        out_specs=(anywhere, anywhere, anywhere, vmem),
+        scratch_shapes=[
+            buf(TOK, D), buf(TOK, D), buf(TOK, D), buf(TOK, FF), buf(FB, D),
+            sem((PIECES + 4,)), sem((PIECES + 3,)),
+        ],
+        compiler_params=pltpu.CompilerParams(vmem_limit_bytes=64 * 1024 * 1024 - 65536),
+        name="finish",
+    )(picked, gate_row, out_grad, hidden_grad, weight_grad)
     return mixed, hidden_grad, weight_grad, gate_grad.reshape(TOK)
 
 

time: 158 us -> 148 us (0.937)
  local copies, waits for them, and re-layouts: 13.3 us -> 0 us
  Pallas kernels: 143 us -> 148 us
    unnamed x6 -> x0, local copies, waits for them, and re-layouts: 12.7 us -> none
    pallas_call x0 -> x1, Pallas kernels: none -> 9.13 us  [layer(): pl.pallas_call(finish, out_shape=(jax.ShapeDtypeStruct((TOK, D), BF), jax...]
    pallas_call x1, Pallas kernels: 143 us -> 138 us  [layer(): pl.pallas_call(kernel, out_shape=(jax.ShapeDtypeStruct((TOK, D), BF), jax...]
where the time goes in v2:
time: 148 us
  Pallas kernels  148 us (100%)
    pallas_call x1, Pallas kernels, layer(): pl.pallas_call(kernel, out_shape=(jax.ShapeDtypeStruct((TOK, D), BF), jax...  138 us
    pallas_call x1, Pallas kernels, layer(): pl.pallas_call(finish, out_shape=(jax.ShapeDtypeStruct((TOK, D), BF), jax...  9.13 us

profile of v2, /device:TPU:1, one launch (start us, length us, event | category | flops | bytes accessed | tf_op | source)
XLA Modules:
  0.0 148.2 jit_solution(8058850065772737031)
XLA Ops:
  0.6 138.4 %experts.1 = (bf16[128,4096]{1,0:T(8,128)(2,1)}, bf16[128,7168]{1,0:T(8,128)(2,1)}, bf16[896,4096]{1,0:T(8,128)(2,1)}) custom-call(bf16[128,7168]{1,0:T(8,128)(2,1)} %hid.1, bf16[896,4096]{1,0:T(8,128)(2,1)} %w_hbm.1, f32[1,128]{1,0:T(1,128)} %bitcast.4, s32[1,128]{1,0:T(1,128)} %bitcast.6, s32[1,128]{1,0:T(1,128)} %bitcast.7, bf16[128,4096]{1,0:T(8,128)(2,1)} %og_hbm.3), custom_call_target="tpu_custom_call" | custom-call | flops 28185722880 | bytes 20000000 | tf_op jit(solution)/shard_map/experts/pallas_call | solution.py:544
  139.1 9.1 %finish.1 = (bf16[128,4096]{1,0:T(8,128)(2,1)}, bf16[128,7168]{1,0:T(8,128)(2,1)}, bf16[896,4096]{1,0:T(8,128)(2,1)}, f32[1,128]{1,0:T(1,128)}) custom-call(bf16[128,4096]{1,0:T(8,128)(2,1)} %get-tuple-element.11.picked_hbm, f32[1,128]{1,0:T(1,128)} %bitcast.5, bf16[128,4096]{1,0:T(8,128)(2,1)} %og_hbm.3, bf16[128,7168]{1,0:T(8,128)(2,1)} %get-tuple-element.12.hg_in, ...), custom_call_target="tpu_custom_call" | custom-call | tf_op jit(solution)/shard_map/finish/pallas_call | solution.py:609

commit v3 on v2

--- a/solution.py
+++ b/solution.py
@@ -54,10 +54,10 @@
 def kernel(
     hid, w_hbm, gates, group_ids, slot_ids, og_hbm,
     picked, hg, wg,
-    wv, h, hxr, cot, cxp, xh, sm, sx, tok, tsend, gm, gx, pa, prcv, r1, r2, ex, em, exr, hp, hpx, rm, rx, kk, og,
+    wv, h, hxr, cot, cxp, xh, sm, sx, tok, tsend, gm, gx, pa, prcv, r1, r2, em, exr, hp, rm, rx, og,
     mt, xb, posv,
     pos_s, pos_r, hz_s, hz_r, w_sem, og_sem, st_sem, t_s, t_r, cm_s, cm_r, cx_s, cx_r, hm_s, hm_r,
-    ag_s, ag_r, agf_s, agf_r, sib_s, sib_r, po_s, po_r, rs_s, rs_r, ret_s, ret_r, eo_s, eo_r, k_s, k_r, hg_s, hg_r, wg_sem,
+    ag_s, ag_r, agf_s, agf_r, sib_s, sib_r, po_s, po_r, rs_s, rs_r, ret_s, ret_r, eo_s, eo_r, k_s, k_r, hg_s, hg_r,
 ):
     g = lax.axis_index("grp")
     z = lax.axis_index("exp")
@@ -73,6 +73,7 @@
     up = (g, zp)
     down = (g, zm)
     blk = c * 4 + z
+    kk, hpx, ex = tok, sx, gx
 
     def plane(i, j):
         p2 = lax.rem(x + i, 4) * 4 + lax.rem(y + j, 4)
@@ -249,7 +250,11 @@
     drain(other_half(z), sib_r.at[z])
     slot_grads(z)
 
-    mine_out = pa.at[c]
+    mine_out = pa
+
+    def other_out(zz):
+        return wg.at[pl.ds(mult(lax.div(zz, 2) * ROWS, 16), ROWS), cols(lax.rem(zz, 2) * HD, HD)]
+
     drain(hxr, hm_r.at[4])
     swap = one(
         (iota((MAIN, MAIN), 0) // 64 == (iota((MAIN, MAIN), 1) // 4) % 4)
@@ -275,11 +280,17 @@
         drain(prcv.at[pl.ds(mult(zz * ROWS, 16), ROWS)], po_r.at[zz])
         add_into(zz, 0, HD, lambda i: prcv.at[pl.ds(mult(zz * ROWS + i * 32, 16), 32)])
 
-    def out_block(zz, start):
-        return mine_out.at[pl.ds(mult(zz * ROWS, 16), ROWS), pl.ds(start, QD)]
-
-    def r2_half(n, start):
-        return r2.at[n, :, pl.ds(start, QD)]
+    def sum_block(zz, n, s):
+        return mine_out.at[pl.ds(mult(zz * ROWS, 16), ROWS), pl.ds(n * QD + s * XD, XD)]
+
+    def r1_block(n, s):
+        return r1.at[n, :, pl.ds(s * XD, XD)]
+
+    def r2_block(side, n, s):
+        return r2.at[side, :, pl.ds(n * QD + s * XD, XD)]
+
+    def send_sum(src, dst, kind, s, dev):
+        remote(src, dst, rs_s.at[2 * kind + s], rs_r.at[2 * kind + s], dev).start()
 
     def partials(k, _):
         zz = order(k)
@@ -297,31 +308,31 @@
         drain(h.at[pl.ds(mult(zz * ROWS, 16), MAIN)], hm_r.at[zz])
         rows_in = h[at, :]
 
-        def product(half):
+        def product(out, part):
             def tile(j, _):
-                pa[half, at, cols(j * QD, QD)] = dot(
-                    rows_in, wv[:, cols(half * HD + j * QD, QD)]
+                out[:, cols(j * QD, QD)] = dot(
+                    rows_in, wv[:, cols(part * HD + j * QD, QD)]
                 ).astype(BF)
                 return 0
 
             lax.fori_loop(0, 2, tile, 0)
 
-        product(nc)
-        remote(
-            pa.at[nc, at], prcv.at[at], po_s.at[zz], po_r.at[zz], sib
-        ).start()
-        product(c)
+        product(other_out(zz), nc)
+        remote(other_out(zz), prcv.at[at], po_s.at[zz], po_r.at[zz], sib).start()
+        product(mine_out.at[at], c)
 
         @pl.when(k == 1)
         def _():
             add_cores(zo)
-            remote(out_block(zo, 0), r1.at[0], rs_s.at[0], rs_r.at[0], up).start()
-            remote(out_block(zo, QD), r1.at[1], rs_s.at[1], rs_r.at[1], down).start()
+            for s in range(2):
+                send_sum(sum_block(zo, 0, s), r1_block(0, s), 0, s, up)
+                send_sum(sum_block(zo, 1, s), r1_block(1, s), 1, s, down)
 
         @pl.when(k == 2)
         def _():
             add_cores(zp)
-            remote(out_block(zp, QD), r2_half(0, QD), rs_s.at[2], rs_r.at[2], up).start()
+            for s in range(2):
+                send_sum(sum_block(zp, 1, s), r2_block(0, 1, s), 2, s, up)
             drain(cot_block(zm, QD, QD), ag_r.at[2])
             to_sibling(zm)
             drain(cot_block(zp, 0, QD), ag_r.at[1])
@@ -330,7 +341,8 @@
         @pl.when(k == 3)
         def _():
             add_cores(zm)
-            remote(out_block(zm, 0), r2_half(1, 0), rs_s.at[3], rs_r.at[3], down).start()
+            for s in range(2):
+                send_sum(sum_block(zm, 0, s), r2_block(1, 0, s), 3, s, down)
 
         return 0
 
@@ -357,35 +369,30 @@
         & ((iota((MAIN, MAIN), 1) // 4) % 16 == iota((MAIN, MAIN), 0) // 16)
         & (iota((MAIN, MAIN), 1) % 4 == iota((MAIN, MAIN), 0) % 4)
     )
+    drain(hp.at[pl.ds(0, 240)], hm_s.at[4])
     hpx[...] = sum(
         dot(unswap[:, zz * EXT : (zz + 1) * EXT], hp[zz * ROWS + MAIN : (zz + 1) * ROWS, :])
         for zz in range(NZ)
     ).astype(BF)
     send_slots(lambda p2: rows(hpx, p2 * 16, 16), rows(rx, p * 16, 16), ret_s.at[4], ret_r.at[4])
 
-    drain(r1.at[0], rs_r.at[0])
-    add_into(zp, 0, QD, lambda i: r1.at[0, pl.ds(mult(i * 32, 16), 32)])
-    remote(out_block(zp, 0), r2_half(0, 0), rs_s.at[4], rs_r.at[4], up).start()
-    drain(r1.at[1], rs_r.at[1])
-    add_into(zm, QD, QD, lambda i: r1.at[1, pl.ds(mult(i * 32, 16), 32)])
-    remote(out_block(zm, QD), r2_half(1, QD), rs_s.at[5], rs_r.at[5], down).start()
+    for s in range(2):
+        for n, zz, dev in ((0, zp, up), (1, zm, down)):
+            drain(r1_block(n, s), rs_r.at[2 * n + s])
+            add_into(
+                zz,
+                n * QD + s * XD,
+                XD,
+                lambda i: r1.at[n, pl.ds(mult(i * 32, 16), 32), pl.ds(s * XD, XD)],
+            )
+            send_sum(sum_block(zz, n, s), r2_block(n, n, s), 4 + n, s, dev)
 
     for zz in range(NZ):
-        drain(pa.at[0, 0:ROWS], po_s.at[zz])
-
-    def weight_tile(j):
-        src = pa.at[nc, pl.ds(0, FB), cols(lax.rem(j, 4) * XD, XD)]
-        return src, local(src, wg.at[:, cols(j * XD, XD)], wg_sem.at[lax.rem(j, 4)])
+        drain(prcv.at[0:ROWS], po_s.at[zz])
 
     def weight_grads(j, _):
-        src, copy = weight_tile(j)
-
-        @pl.when(j >= 4)
-        def _():
-            copy.wait()
-
-        src[...] = dot_tn(h[...], cot[:, cols(j * XD, XD)]).astype(BF)
-        copy.start()
+        at = cols(j * XD, XD)
+        wg[:, at] = dot_tn(h[...], cot[:, at]).astype(BF)
         return 0
 
     lax.fori_loop(0, 8, weight_grads, 0)
@@ -403,132 +410,127 @@
 
     lax.fori_loop(0, NZ, tokens_grad, 0)
 
-    drain(r2_half(0, 0), rs_r.at[4])
-    drain(r2_half(0, QD), rs_r.at[2])
-    drain(r2_half(1, 0), rs_r.at[3])
-    drain(r2_half(1, QD), rs_r.at[5])
-
-    def last_sum(first, count, start, size):
-        def step(i, _):
-            from_row = first + i * 32
-            at = pl.ds(mult(z * ROWS + from_row, 16), 32)
-            there = pl.ds(mult(from_row, 16), 32)
-            where = pl.ds(start, size)
-            mine_out[at, where] = (
-                mine_out[at, where].astype(F32)
-                + r2[0, there, where].astype(F32)
-                + r2[1, there, where].astype(F32)
-            ).astype(BF)
-            return 0
-
-        lax.fori_loop(0, count // 32, step, 0)
-
-    last_sum(MAIN, EXT, 0, HD)
-    back = (iota((MAIN, EXT), 1) // 4 == iota((MAIN, EXT), 0) // 16) & (
-        iota((MAIN, EXT), 1) % 4 == iota((MAIN, EXT), 0) % 4
-    )
-    tail = mine_out[pl.ds(mult(z * ROWS + MAIN, 16), EXT), :]
-    ex[...] = sum(
-        dot(one(back & ((iota((MAIN, EXT), 0) // 4) % 4 == q)), tail[:, q * XD : (q + 1) * XD])
-        for q in range(4)
-    ).astype(BF)
-    send_slots(lambda p2: rows(ex, p2 * 16, 16), rows(exr, p * 16, 16), eo_s.at[2], eo_r.at[2])
     for n in range(2):
-        last_sum(0, MAIN, n * QD, QD)
-        send_slots(
-            lambda p2: half(mine_out, z * ROWS + p2 * 16, 16, n),
-            half(em, p * 16, 16, n),
-            eo_s.at[n],
-            eo_r.at[n],
-        )
-
-    def return_grads(piece, _):
+        drain(half(gm, 0, 240, n), cm_s.at[n])
+    drain(gx.at[pl.ds(0, 240)], cx_s.at[0])
+
+    def return_grads(piece):
         for dc, dz in COLUMN:
             c2, z2, dev = column(dc, dz)
             src = rows(xh, (z2 * 2 + c2) * TOK + piece * 32, 32)
             dst = hg.at[pl.ds(mult(piece * 32, 16), 32), cols(blk * FB, FB)]
             remote(src, dst, hg_s.at[0], hg_r.at[0], dev).start()
-        return 0
-
-    lax.fori_loop(0, 4, return_grads, 0)
+
+    def last_sum(first, count, n, s):
+        at = pl.ds(mult(z * ROWS + first, 16), count)
+        there = pl.ds(mult(first, 16), count)
+        where = pl.ds(n * QD + s * XD, XD)
+        return (
+            mine_out[at, where].astype(F32)
+            + r2[0, there, where].astype(F32)
+            + r2[1, there, where].astype(F32)
+        ).astype(BF)
+
+    back = (iota((MAIN, EXT), 1) // 4 == iota((MAIN, EXT), 0) // 16) & (
+        iota((MAIN, EXT), 1) % 4 == iota((MAIN, EXT), 0) % 4
+    )
+    SD = XD // 2
+    for s in range(2):
+        for kind, side, n in ((2, 0, 1), (3, 1, 0), (4, 0, 0), (5, 1, 1)):
+            drain(r2_block(side, n, s), rs_r.at[2 * kind + s])
+        if s == 1:
+            lax.fori_loop(0, 4, lambda piece, _: return_grads(piece) or 0, 0)
+        for n in range(2):
+
+            def main_rows(i, _):
+                at = pl.ds(mult(i * 32, 16), 32)
+                gm[at, (2 * s + n) * XD : (2 * s + n + 1) * XD] = last_sum(i * 32, 32, n, s)
+                return 0
+
+            lax.fori_loop(0, MAIN // 32, main_rows, 0)
+        send_slots(
+            lambda p2: half(gm, p2 * 16, 16, s), half(em, p * 16, 16, s), eo_s.at[s], eo_r.at[s]
+        )
+        tails = [last_sum(MAIN, EXT, n, s) for n in range(2)]
+        ex[:, s * SD : (s + 1) * SD] = sum(
+            dot(
+                one(back & ((iota((MAIN, EXT), 0) // 4) % 4 == q)),
+                tails[q // 2][:, (q % 2) * SD : (q % 2 + 1) * SD],
+            )
+            for q in range(4)
+        ).astype(BF)
+        send_slots(
+            lambda p2: ex.at[pl.ds(mult(p2 * 16, 16), 16), pl.ds(s * SD, SD)],
+            exr.at[pl.ds(mult(p * 16, 16), 16), pl.ds(s * SD, SD)],
+            eo_s.at[2 + s],
+            eo_r.at[2 + s],
+        )
     local(rows(xh, (z * 2 + c) * TOK, TOK), hg.at[:, cols(blk * FB, FB)], hg_r.at[0]).start()
 
-    drain(exr, eo_r.at[2])
-    for n in range(2):
-        drain(half(em, 0, MAIN, n), eo_r.at[n])
-        rows_out = dot_tn(table(z), em[:, n * QD : (n + 1) * QD])
-        late = jnp.concatenate([dot_tn(extra_pick(z, 2 * n + q), exr[...]) for q in range(2)], axis=1)
-        kk[0:TOK, n * QD : (n + 1) * QD] = rows_out[0:TOK, :].astype(BF)
-        kk[TOK : 2 * TOK, n * QD : (n + 1) * QD] = (rows_out[TOK:, :] + late).astype(BF)
-        there = picked.at[:, cols(c * HD + n * QD, QD)]
-        remote(half(kk, nc * TOK, TOK, n), there, k_s.at[n], k_r.at[n], sib).start()
-        local(half(kk, c * TOK, TOK, n), there, k_s.at[2 + n]).start()
-
-    for n in range(2):
-        drain(picked.at[:, cols(nc * HD + n * QD, QD)], k_r.at[n])
-        drain(half(kk, 0, TOK, n), k_s.at[n])
-        drain(half(kk, 0, TOK, n), k_s.at[2 + n])
+    for s in range(2):
+        drain(half(em, 0, MAIN, s), eo_r.at[s])
+        drain(exr.at[:, pl.ds(s * SD, SD)], eo_r.at[2 + s])
+        rows_out = dot_tn(table(z), em[:, s * QD : (s + 1) * QD])
+        late = jnp.concatenate(
+            [dot_tn(extra_pick(z, q), exr[:, s * SD : (s + 1) * SD]) for q in range(4)], axis=1
+        )
+        kk[0:TOK, s * QD : (s + 1) * QD] = rows_out[0:TOK, :].astype(BF)
+        kk[TOK : 2 * TOK, s * QD : (s + 1) * QD] = (rows_out[TOK:, :] + late).astype(BF)
+        for n in range(2):
+            m = 2 * s + n
+            there = picked.at[:, cols(c * HD + n * QD + s * XD, XD)]
+            src = kk.at[pl.ds(mult(nc * TOK, 16), TOK), pl.ds(m * XD, XD)]
+            remote(src, there, k_s.at[m], k_r.at[m], sib).start()
+            src = kk.at[pl.ds(mult(c * TOK, 16), TOK), pl.ds(m * XD, XD)]
+            local(src, there, k_s.at[4 + m]).start()
+
+    for m in range(4):
+        there = picked.at[:, cols(nc * HD + (m % 2) * QD + (m // 2) * XD, XD)]
+        drain(there, k_r.at[m])
+        drain(there, k_s.at[m])
+        drain(there, k_s.at[4 + m])
     drain(hg, hg_r.at[0])
-    for j in range(4):
-        weight_tile(j)[1].wait()
     drain(rows(posv, 0, 56, 8), pos_s.at[0])
     drain(xh.at[pl.ds(0, 7 * TOK)], hg_s.at[0])
     drain(tsend, t_s.at[0])
-    for n in range(2):
-        drain(half(gm, 0, 240, n), cm_s.at[n])
-        drain(half(em, 0, 240, n), eo_s.at[n])
-    drain(gx.at[pl.ds(0, 240)], cx_s.at[0])
+    for s in range(2):
+        drain(half(em, 0, 240, s), eo_s.at[s])
+        drain(exr.at[pl.ds(0, 240), pl.ds(s * SD, SD)], eo_s.at[2 + s])
     for n in range(5):
-        drain(hp.at[pl.ds(0, 240)], hm_s.at[n])
+        if n < 4:
+            drain(hp.at[pl.ds(0, 240)], hm_s.at[n])
         drain(hp.at[pl.ds(0, 240)], ret_s.at[n])
     for n in range(4):
         drain(r1.at[0], ag_s.at[n])
         drain(r2.at[0], sib_s.at[n])
     for n in range(2):
         drain(r1.at[0], agf_s.at[n])
-    for n in range(6):
-        drain(r1.at[0], rs_s.at[n])
-    drain(exr.at[pl.ds(0, 240)], eo_s.at[2])
-
-
-PIECES = 8
-
-
-def finish(
-    picked_hbm, gates, og_hbm, hg_in, wg_in, mixed, hg, wg, gg, picked, og, out, hbuf, wbuf, in_sem, out_sem
-):
-    copies = []
+    for n in range(12):
+        drain(r1_block(0, 0), rs_s.at[n])
+
+
+PIECES = 4
+
+
+def finish(picked, gates, og_hbm, hg_in, wg_in, mixed, hg, wg, gg, og, out, in_sem, out_sem):
+    load = pltpu.make_async_copy(og_hbm, og, in_sem.at[0])
+    load.start()
+    stores = [pltpu.make_async_copy(hg_in, hg, out_sem.at[PIECES])]
     for k in range(PIECES):
         at = pl.ds(k * (FB // PIECES), FB // PIECES)
-        copies.append((wg_in.at[at], wbuf.at[at], wg.at[at]))
-    for k in range(2):
-        at = pl.ds(k * (TOK // 2), TOK // 2)
-        copies.append((hg_in.at[at], hbuf.at[at], hg.at[at]))
-    loads = [pltpu.make_async_copy(a, b, in_sem.at[k]) for k, (a, b, _) in enumerate(copies)]
-    stores = [pltpu.make_async_copy(b, a, out_sem.at[k]) for k, (_, b, a) in enumerate(copies)]
-    rows_in = [
-        pltpu.make_async_copy(picked_hbm, picked, in_sem.at[PIECES + 2]),
-        pltpu.make_async_copy(og_hbm, og, in_sem.at[PIECES + 3]),
-    ]
-    for copy in rows_in + loads:
+        stores.append(pltpu.make_async_copy(wg_in.at[at], wg.at[at], out_sem.at[k]))
+    for copy in stores:
         copy.start()
     eye = iota((TOK, TOK), 0) == iota((TOK, TOK), 1)
     gate = jnp.sum(jnp.where(eye, gates[...], 0.0), axis=1, keepdims=True)
-    for copy in rows_in:
-        copy.wait()
     rows = picked[...].astype(F32)
     out[...] = (gate * rows).astype(BF)
-    store = pltpu.make_async_copy(out, mixed, out_sem.at[PIECES + 2])
-    store.start()
-    for load, copy in zip(loads[:4], stores):
-        load.wait()
-        copy.start()
+    stores.append(pltpu.make_async_copy(out, mixed, out_sem.at[PIECES + 1]))
+    stores[-1].start()
+    load.wait()
     total = jnp.sum(og[...].astype(F32) * rows, axis=1, keepdims=True)
     gg[...] = jnp.sum(jnp.where(eye, total, 0.0), axis=0, keepdims=True)
-    for load, copy in zip(loads[4:], stores[4:]):
-        load.wait()
-        copy.start()
-    for copy in stores + [store]:
+    for copy in stores:
         copy.wait()
 
 
@@ -543,13 +545,9 @@
     gate_row = gates.reshape(1, TOK)
     picked, hidden_grad, weight_grad = pl.pallas_call(
         kernel,
-        out_shape=(
-            jax.ShapeDtypeStruct((TOK, D), BF),
-            jax.ShapeDtypeStruct((TOK, FF), BF),
-            jax.ShapeDtypeStruct((FB, D), BF),
-        ),
+        out_shape=(pltpu.VMEM((TOK, D), BF), pltpu.VMEM((TOK, FF), BF), pltpu.VMEM((FB, D), BF)),
         in_specs=[anywhere, anywhere, vmem, vmem, vmem, anywhere],
-        out_specs=(anywhere, anywhere, anywhere),
+        out_specs=(vmem, vmem, vmem),
         scratch_shapes=[
             buf(FB, D),
             buf(NZ * ROWS, FB),
@@ -563,18 +561,15 @@
             buf(TOK, HD),
             buf(MAIN, HD),
             buf(MAIN, XD),
-            buf(2, NZ * ROWS, HD),
+            buf(NZ * ROWS, HD),
             buf(NZ * ROWS, HD),
             buf(2, ROWS, QD),
             buf(2, ROWS, HD),
-            buf(MAIN, XD),
             buf(MAIN, HD),
             buf(MAIN, XD),
             buf(NZ * ROWS, FB),
-            buf(MAIN, FB),
             buf(NZ * MAIN, FB),
             buf(MAIN, FB),
-            buf(2 * TOK, HD),
             buf(TOK, D),
             buf(NZ * MAIN, 2 * TOK),
             buf(NZ * MAIN, TOK),
@@ -590,15 +585,14 @@
             sem((2,)), sem((2,)),
             sem((4,)), sem((4,)),
             sem((4,)), sem((4,)),
-            sem((6,)), sem((6,)),
+            sem((12,)), sem((12,)),
             sem((5,)), sem((5,)),
-            sem((3,)), sem((3,)),
-            sem((4,)), sem((2,)),
+            sem((4,)), sem((4,)),
+            sem((8,)), sem((4,)),
             sem((1,)), sem((1,)),
-            sem((4,)),
         ],
         compiler_params=pltpu.CompilerParams(
-            collective_id=0, has_side_effects=True, vmem_limit_bytes=64 * 1024 * 1024 - 65536
+            collective_id=0, has_side_effects=True, vmem_limit_bytes=54 * 1024 * 1024 - 65536
         ),
         cost_estimate=pl.CostEstimate(
             flops=6 * NZ * ROWS * FB * D, bytes_accessed=20_000_000, transcendentals=0
@@ -606,6 +600,10 @@
         name="experts",
     )(hidden_in, weights, gate_row, group_ids.reshape(1, TOK), slot_ids.reshape(1, TOK), out_grad)
 
+    results = [
+        pltpu.with_memory_space_constraint(value, pltpu.VMEM)
+        for value in (picked, hidden_grad, weight_grad)
+    ]
     mixed, hidden_grad, weight_grad, gate_grad = pl.pallas_call(
         finish,
         out_shape=(
@@ -614,15 +612,12 @@
             jax.ShapeDtypeStruct((FB, D), BF),
             jax.ShapeDtypeStruct((1, TOK), F32),
         ),
-        in_specs=[anywhere, vmem, anywhere, anywhere, anywhere],
+        in_specs=[vmem, vmem, anywhere, vmem, vmem],
         out_specs=(anywhere, anywhere, anywhere, vmem),
-        scratch_shapes=[
-            buf(TOK, D), buf(TOK, D), buf(TOK, D), buf(TOK, FF), buf(FB, D),
-            sem((PIECES + 4,)), sem((PIECES + 3,)),
-        ],
-        compiler_params=pltpu.CompilerParams(vmem_limit_bytes=64 * 1024 * 1024 - 65536),
+        scratch_shapes=[buf(TOK, D), buf(TOK, D), sem((1,)), sem((PIECES + 2,))],
+        compiler_params=pltpu.CompilerParams(vmem_limit_bytes=52 * 1024 * 1024),
         name="finish",
-    )(picked, gate_row, out_grad, hidden_grad, weight_grad)
+    )(results[0], gate_row, out_grad, results[1], results[2])
     return mixed, hidden_grad, weight_grad, gate_grad.reshape(TOK)
 
 

time: 148 us -> 143 us (0.966)
  Pallas kernels: 148 us -> 142 us
    pallas_call x1, Pallas kernels: 9.13 us -> 5.11 us  [layer(): pl.pallas_call(finish, out_shape=(jax.ShapeDtypeStruct((TOK, D), BF), jax...]
where the time goes in v3:
time: 143 us
  Pallas kernels  142 us (99%)
    pallas_call x1, Pallas kernels, layer(): pl.pallas_call(kernel, out_shape=(pltpu.VMEM((TOK, D), BF), pltpu.VMEM((T...  137 us
    pallas_call x1, Pallas kernels, layer(): pl.pallas_call(finish, out_shape=(jax.ShapeDtypeStruct((TOK, D), BF), jax...  5.11 us

profile of v3, /device:TPU:1, one launch (start us, length us, event | category | flops | bytes accessed | tf_op | source)
XLA Modules:
  0.0 142.8 jit_solution(5099371415020414889)
XLA Ops:
  0.6 137.1 %experts.1 = (bf16[128,4096]{1,0:T(8,128)(2,1)S(1)}, bf16[128,7168]{1,0:T(8,128)(2,1)S(1)}, bf16[896,4096]{1,0:T(8,128)(2,1)S(1)}) custom-call(bf16[128,7168]{1,0:T(8,128)(2,1)} %hid.1, bf16[896,4096]{1,0:T(8,128)(2,1)} %w_hbm.1, f32[1,128]{1,0:T(1,128)} %bitcast.4, s32[1,128]{1,0:T(1,128)} %bitcast.6, s32[1,128]{1,0:T(1,128)} %bitcast.7, ...), custom_call_target="tpu_custom_call" | custom-call | flops 28185722880 | bytes 20000000 | tf_op jit(solution)/shard_map/experts/pallas_call | solution.py:546
  137.7 5.1 %finish.1 = (bf16[128,4096]{1,0:T(8,128)(2,1)}, bf16[128,7168]{1,0:T(8,128)(2,1)}, bf16[896,4096]{1,0:T(8,128)(2,1)}, f32[1,128]{1,0:T(1,128)}) custom-call(bf16[128,4096]{1,0:T(8,128)(2,1)S(1)} %get-tuple-element.11.picked, f32[1,128]{1,0:T(1,128)} %bitcast.5, bf16[128,4096]{1,0:T(8,128)(2,1)} %og_hbm.3, bf16[128,7168]{1,0:T(8,128)(2,1)S(1)} %get-tuple-element.12.hg_in, ...), custom_call_target="tpu_custom_call" | custom-call | tf_op jit(solution)/shard_map/finish/pallas_call | solution.py:607

commit v4 on v3

--- a/solution.py
+++ b/solution.py
@@ -53,8 +53,8 @@
 
 def kernel(
     hid, w_hbm, gates, group_ids, slot_ids, og_hbm,
-    picked, hg, wg,
-    wv, h, hxr, cot, cxp, xh, sm, sx, tok, tsend, gm, gx, pa, prcv, r1, r2, em, exr, hp, rm, rx, og,
+    mixed, hg, wg, gg,
+    wv, h, hxr, cot, cxp, xh, sm, sx, tok, tsend, gm, gx, pa, prcv, r1, r2, hp, rm, rx, kr, og,
     mt, xb, posv,
     pos_s, pos_r, hz_s, hz_r, w_sem, og_sem, st_sem, t_s, t_r, cm_s, cm_r, cx_s, cx_r, hm_s, hm_r,
     ag_s, ag_r, agf_s, agf_r, sib_s, sib_r, po_s, po_r, rs_s, rs_r, ret_s, ret_r, eo_s, eo_r, k_s, k_r, hg_s, hg_r,
@@ -73,7 +73,7 @@
     up = (g, zp)
     down = (g, zm)
     blk = c * 4 + z
-    kk, hpx, ex = tok, sx, gx
+    kk, hpx, ex, em, exr = prcv, sx, gx, tok, cxp
 
     def plane(i, j):
         p2 = lax.rem(x + i, 4) * 4 + lax.rem(y + j, 4)
@@ -438,8 +438,7 @@
     for s in range(2):
         for kind, side, n in ((2, 0, 1), (3, 1, 0), (4, 0, 0), (5, 1, 1)):
             drain(r2_block(side, n, s), rs_r.at[2 * kind + s])
-        if s == 1:
-            lax.fori_loop(0, 4, lambda piece, _: return_grads(piece) or 0, 0)
+        lax.fori_loop(2 * s, 2 + 2 * s, lambda piece, _: return_grads(piece) or 0, 0)
         for n in range(2):
 
             def main_rows(i, _):
@@ -476,19 +475,23 @@
         )
         kk[0:TOK, s * QD : (s + 1) * QD] = rows_out[0:TOK, :].astype(BF)
         kk[TOK : 2 * TOK, s * QD : (s + 1) * QD] = (rows_out[TOK:, :] + late).astype(BF)
-        for n in range(2):
-            m = 2 * s + n
-            there = picked.at[:, cols(c * HD + n * QD + s * XD, XD)]
-            src = kk.at[pl.ds(mult(nc * TOK, 16), TOK), pl.ds(m * XD, XD)]
-            remote(src, there, k_s.at[m], k_r.at[m], sib).start()
-            src = kk.at[pl.ds(mult(c * TOK, 16), TOK), pl.ds(m * XD, XD)]
-            local(src, there, k_s.at[4 + m]).start()
-
-    for m in range(4):
-        there = picked.at[:, cols(nc * HD + (m % 2) * QD + (m // 2) * XD, XD)]
-        drain(there, k_r.at[m])
-        drain(there, k_s.at[m])
-        drain(there, k_s.at[4 + m])
+        src = kk.at[pl.ds(mult(nc * TOK, 16), TOK), pl.ds(s * QD, QD)]
+        remote(src, kr.at[:, pl.ds(s * QD, QD)], k_s.at[s], k_r.at[s], sib).start()
+
+    total = jnp.zeros((TOK, 1), F32)
+    for core, ref, first in ((c, kk, mult(c * TOK, 16)), (nc, kr, 0)):
+        for s in range(2):
+            if ref is kr:
+                drain(kr.at[:, pl.ds(s * QD, QD)], k_r.at[s])
+            for n in range(2):
+                at = cols(core * HD + n * QD + s * XD, XD)
+                picked = ref[pl.ds(first, TOK), (2 * s + n) * XD : (2 * s + n + 1) * XD].astype(F32)
+                total += jnp.sum(og[:, at].astype(F32) * picked, axis=1, keepdims=True)
+                mixed[:, at] = (gate * picked).astype(BF)
+    gg[...] = jnp.sum(jnp.where(eye, total, 0.0), axis=0, keepdims=True)
+
+    for s in range(2):
+        drain(kr.at[:, pl.ds(s * QD, QD)], k_s.at[s])
     drain(hg, hg_r.at[0])
     drain(rows(posv, 0, 56, 8), pos_s.at[0])
     drain(xh.at[pl.ds(0, 7 * TOK)], hg_s.at[0])
@@ -512,25 +515,15 @@
 PIECES = 4
 
 
-def finish(picked, gates, og_hbm, hg_in, wg_in, mixed, hg, wg, gg, og, out, in_sem, out_sem):
-    load = pltpu.make_async_copy(og_hbm, og, in_sem.at[0])
-    load.start()
-    stores = [pltpu.make_async_copy(hg_in, hg, out_sem.at[PIECES])]
+def finish(mixed_in, hg_in, wg_in, gg_in, mixed, hg, wg, gg, sems):
+    copies = [(mixed_in, mixed), (hg_in, hg), (gg_in, gg)]
     for k in range(PIECES):
         at = pl.ds(k * (FB // PIECES), FB // PIECES)
-        stores.append(pltpu.make_async_copy(wg_in.at[at], wg.at[at], out_sem.at[k]))
-    for copy in stores:
+        copies.append((wg_in.at[at], wg.at[at]))
+    copies = [pltpu.make_async_copy(a, b, sems.at[k]) for k, (a, b) in enumerate(copies)]
+    for copy in copies:
         copy.start()
-    eye = iota((TOK, TOK), 0) == iota((TOK, TOK), 1)
-    gate = jnp.sum(jnp.where(eye, gates[...], 0.0), axis=1, keepdims=True)
-    rows = picked[...].astype(F32)
-    out[...] = (gate * rows).astype(BF)
-    stores.append(pltpu.make_async_copy(out, mixed, out_sem.at[PIECES + 1]))
-    stores[-1].start()
-    load.wait()
-    total = jnp.sum(og[...].astype(F32) * rows, axis=1, keepdims=True)
-    gg[...] = jnp.sum(jnp.where(eye, total, 0.0), axis=0, keepdims=True)
-    for copy in stores:
+    for copy in copies:
         copy.wait()
 
 
@@ -543,11 +536,16 @@
         return pltpu.VMEM(shape, BF)
 
     gate_row = gates.reshape(1, TOK)
-    picked, hidden_grad, weight_grad = pl.pallas_call(
+    results = pl.pallas_call(
         kernel,
-        out_shape=(pltpu.VMEM((TOK, D), BF), pltpu.VMEM((TOK, FF), BF), pltpu.VMEM((FB, D), BF)),
+        out_shape=(
+            pltpu.VMEM((TOK, D), BF),
+            pltpu.VMEM((TOK, FF), BF),
+            pltpu.VMEM((FB, D), BF),
+            pltpu.VMEM((1, TOK), F32),
+        ),
         in_specs=[anywhere, anywhere, vmem, vmem, vmem, anywhere],
-        out_specs=(vmem, vmem, vmem),
+        out_specs=(vmem, vmem, vmem, vmem),
         scratch_shapes=[
             buf(FB, D),
             buf(NZ * ROWS, FB),
@@ -565,11 +563,10 @@
             buf(NZ * ROWS, HD),
             buf(2, ROWS, QD),
             buf(2, ROWS, HD),
-            buf(MAIN, HD),
-            buf(MAIN, XD),
             buf(NZ * ROWS, FB),
             buf(NZ * MAIN, FB),
             buf(MAIN, FB),
+            buf(TOK, HD),
             buf(TOK, D),
             buf(NZ * MAIN, 2 * TOK),
             buf(NZ * MAIN, TOK),
@@ -588,11 +585,11 @@
             sem((12,)), sem((12,)),
             sem((5,)), sem((5,)),
             sem((4,)), sem((4,)),
-            sem((8,)), sem((4,)),
+            sem((2,)), sem((2,)),
             sem((1,)), sem((1,)),
         ],
         compiler_params=pltpu.CompilerParams(
-            collective_id=0, has_side_effects=True, vmem_limit_bytes=54 * 1024 * 1024 - 65536
+            collective_id=0, has_side_effects=True, vmem_limit_bytes=55104 * 1024
         ),
         cost_estimate=pl.CostEstimate(
             flops=6 * NZ * ROWS * FB * D, bytes_accessed=20_000_000, transcendentals=0
@@ -600,10 +597,7 @@
         name="experts",
     )(hidden_in, weights, gate_row, group_ids.reshape(1, TOK), slot_ids.reshape(1, TOK), out_grad)
 
-    results = [
-        pltpu.with_memory_space_constraint(value, pltpu.VMEM)
-        for value in (picked, hidden_grad, weight_grad)
-    ]
+    results = [pltpu.with_memory_space_constraint(value, pltpu.VMEM) for value in results]
     mixed, hidden_grad, weight_grad, gate_grad = pl.pallas_call(
         finish,
         out_shape=(
@@ -612,12 +606,12 @@
             jax.ShapeDtypeStruct((FB, D), BF),
             jax.ShapeDtypeStruct((1, TOK), F32),
         ),
-        in_specs=[vmem, vmem, anywhere, vmem, vmem],
-        out_specs=(anywhere, anywhere, anywhere, vmem),
-        scratch_shapes=[buf(TOK, D), buf(TOK, D), sem((1,)), sem((PIECES + 2,))],
-        compiler_params=pltpu.CompilerParams(vmem_limit_bytes=52 * 1024 * 1024),
+        in_specs=[vmem, vmem, vmem, vmem],
+        out_specs=(anywhere, anywhere, anywhere, anywhere),
+        scratch_shapes=[sem((PIECES + 3,))],
+        compiler_params=pltpu.CompilerParams(vmem_limit_bytes=40 * 1024 * 1024),
         name="finish",
-    )(results[0], gate_row, out_grad, results[1], results[2])
+    )(*results)
     return mixed, hidden_grad, weight_grad, gate_grad.reshape(TOK)
 
 

time: 143 us -> 141 us (0.986)
  no operation moved by 1% of the time
where the time goes in v4:
time: 141 us
  Pallas kernels  141 us (100%)
    pallas_call x1, Pallas kernels, layer(): pl.pallas_call(kernel, out_shape=(pltpu.VMEM((TOK, D), BF), pltpu.VMEM((T...  137 us
    pallas_call x1, Pallas kernels, layer(): pl.pallas_call(finish, out_shape=(jax.ShapeDtypeStruct((TOK, D), BF), jax...  3.95 us

profile of v4, /device:TPU:1, one launch (start us, length us, event | category | flops | bytes accessed | tf_op | source)
XLA Modules:
  0.0 141.3 jit_solution(14196099850158530626)
XLA Ops:
  0.6 136.7 %experts.1 = (bf16[128,4096]{1,0:T(8,128)(2,1)S(1)}, bf16[128,7168]{1,0:T(8,128)(2,1)S(1)}, bf16[896,4096]{1,0:T(8,128)(2,1)S(1)}, f32[1,128]{1,0:T(1,128)S(1)}) custom-call(bf16[128,7168]{1,0:T(8,128)(2,1)} %hid.1, bf16[896,4096]{1,0:T(8,128)(2,1)} %w_hbm.1, f32[1,128]{1,0:T(1,128)} %bitcast.4, s32[1,128]{1,0:T(1,128)} %bitcast.5, s32[1,128]{1,0:T(1,128)} %bitcast.6, ...), custom_call_target="tpu_custom_call" | custom-call | flops 28185722880 | bytes 20000000 | tf_op jit(solution)/shard_map/experts/pallas_call | solution.py:539
  137.3 4.0 %finish.1 = (bf16[128,4096]{1,0:T(8,128)(2,1)}, bf16[128,7168]{1,0:T(8,128)(2,1)}, bf16[896,4096]{1,0:T(8,128)(2,1)}, f32[1,128]{1,0:T(1,128)}) custom-call(bf16[128,4096]{1,0:T(8,128)(2,1)S(1)} %get-tuple-element.12.mixed_in, bf16[128,7168]{1,0:T(8,128)(2,1)S(1)} %get-tuple-element.13.hg_in, bf16[896,4096]{1,0:T(8,128)(2,1)S(1)} %get-tuple-element.14.wg_in, ...), custom_call_target="tpu_custom_call" | custom-call | tf_op jit(solution)/shard_map/finish/pallas_call | solution.py:601

commit v5 on v4

--- a/solution.py
+++ b/solution.py
@@ -362,7 +362,20 @@
         slot_grads(zz)
         return 0
 
-    lax.fori_loop(0, 3, more_grads, 0)
+    lax.fori_loop(0, 2, more_grads, 0)
+
+    for s in range(2):
+        for n, zz, dev in ((0, zp, up), (1, zm, down)):
+            drain(r1_block(n, s), rs_r.at[2 * n + s])
+            add_into(
+                zz,
+                n * QD + s * XD,
+                XD,
+                lambda i: r1.at[n, pl.ds(mult(i * 32, 16), 32), pl.ds(s * XD, XD)],
+            )
+            send_sum(sum_block(zz, n, s), r2_block(n, n, s), 4 + n, s, dev)
+
+    more_grads(jnp.int32(2), 0)
 
     unswap = one(
         (iota((MAIN, MAIN), 1) // 64 == (iota((MAIN, MAIN), 0) // 4) % 4)
@@ -375,17 +388,6 @@
         for zz in range(NZ)
     ).astype(BF)
     send_slots(lambda p2: rows(hpx, p2 * 16, 16), rows(rx, p * 16, 16), ret_s.at[4], ret_r.at[4])
-
-    for s in range(2):
-        for n, zz, dev in ((0, zp, up), (1, zm, down)):
-            drain(r1_block(n, s), rs_r.at[2 * n + s])
-            add_into(
-                zz,
-                n * QD + s * XD,
-                XD,
-                lambda i: r1.at[n, pl.ds(mult(i * 32, 16), 32), pl.ds(s * XD, XD)],
-            )
-            send_sum(sum_block(zz, n, s), r2_block(n, n, s), 4 + n, s, dev)
 
     for zz in range(NZ):
         drain(prcv.at[0:ROWS], po_s.at[zz])

time: 141 us -> 142 us (level)
  no operation moved by 1% of the time
where the time goes in v5:
time: 142 us; the launch traced here: 141 us
  Pallas kernels  141 us (99%)
    pallas_call x1, Pallas kernels, layer(): pl.pallas_call(kernel, out_shape=(pltpu.VMEM((TOK, D), BF), pltpu.VMEM((T...  137 us
    pallas_call x1, Pallas kernels, layer(): pl.pallas_call(finish, out_shape=(jax.ShapeDtypeStruct((TOK, D), BF), jax...  3.95 us

profile of v5, /device:TPU:1, one launch (start us, length us, event | category | flops | bytes accessed | tf_op | source)
XLA Modules:
  0.0 141.4 jit_solution(4602220070874959344)
XLA Ops:
  0.6 136.7 %experts.1 = (bf16[128,4096]{1,0:T(8,128)(2,1)S(1)}, bf16[128,7168]{1,0:T(8,128)(2,1)S(1)}, bf16[896,4096]{1,0:T(8,128)(2,1)S(1)}, f32[1,128]{1,0:T(1,128)S(1)}) custom-call(bf16[128,7168]{1,0:T(8,128)(2,1)} %hid.1, bf16[896,4096]{1,0:T(8,128)(2,1)} %w_hbm.1, f32[1,128]{1,0:T(1,128)} %bitcast.4, s32[1,128]{1,0:T(1,128)} %bitcast.5, s32[1,128]{1,0:T(1,128)} %bitcast.6, ...), custom_call_target="tpu_custom_call" | custom-call | flops 28185722880 | bytes 20000000 | tf_op jit(solution)/shard_map/experts/pallas_call | solution.py:541
  137.3 4.0 %finish.1 = (bf16[128,4096]{1,0:T(8,128)(2,1)}, bf16[128,7168]{1,0:T(8,128)(2,1)}, bf16[896,4096]{1,0:T(8,128)(2,1)}, f32[1,128]{1,0:T(1,128)}) custom-call(bf16[128,4096]{1,0:T(8,128)(2,1)S(1)} %get-tuple-element.12.mixed_in, bf16[128,7168]{1,0:T(8,128)(2,1)S(1)} %get-tuple-element.13.hg_in, bf16[896,4096]{1,0:T(8,128)(2,1)S(1)} %get-tuple-element.14.wg_in, ...), custom_call_target="tpu_custom_call" | custom-call | tf_op jit(solution)/shard_map/finish/pallas_call | solution.py:603

commit v6 on v4

--- a/solution.py
+++ b/solution.py
@@ -435,10 +435,12 @@
         iota((MAIN, EXT), 1) % 4 == iota((MAIN, EXT), 0) % 4
     )
     SD = XD // 2
+    lax.fori_loop(0, 2, lambda piece, _: return_grads(piece) or 0, 0)
     for s in range(2):
         for kind, side, n in ((2, 0, 1), (3, 1, 0), (4, 0, 0), (5, 1, 1)):
             drain(r2_block(side, n, s), rs_r.at[2 * kind + s])
-        lax.fori_loop(2 * s, 2 + 2 * s, lambda piece, _: return_grads(piece) or 0, 0)
+        if s == 1:
+            lax.fori_loop(2, 4, lambda piece, _: return_grads(piece) or 0, 0)
         for n in range(2):
 
             def main_rows(i, _):

time: 141 us -> 141 us (level)
  no operation moved by 1% of the time
where the time goes in v6:
time: 141 us
  Pallas kernels  141 us (100%)
    pallas_call x1, Pallas kernels, layer(): pl.pallas_call(kernel, out_shape=(pltpu.VMEM((TOK, D), BF), pltpu.VMEM((T...  137 us
    pallas_call x1, Pallas kernels, layer(): pl.pallas_call(finish, out_shape=(jax.ShapeDtypeStruct((TOK, D), BF), jax...  3.95 us

profile of v6, /device:TPU:1, one launch (start us, length us, event | category | flops | bytes accessed | tf_op | source)
XLA Modules:
  0.0 141.3 jit_solution(10518083748879918053)
XLA Ops:
  0.6 136.7 %experts.1 = (bf16[128,4096]{1,0:T(8,128)(2,1)S(1)}, bf16[128,7168]{1,0:T(8,128)(2,1)S(1)}, bf16[896,4096]{1,0:T(8,128)(2,1)S(1)}, f32[1,128]{1,0:T(1,128)S(1)}) custom-call(bf16[128,7168]{1,0:T(8,128)(2,1)} %hid.1, bf16[896,4096]{1,0:T(8,128)(2,1)} %w_hbm.1, f32[1,128]{1,0:T(1,128)} %bitcast.4, s32[1,128]{1,0:T(1,128)} %bitcast.5, s32[1,128]{1,0:T(1,128)} %bitcast.6, ...), custom_call_target="tpu_custom_call" | custom-call | flops 28185722880 | bytes 20000000 | tf_op jit(solution)/shard_map/experts/pallas_call | solution.py:541
  137.3 4.0 %finish.1 = (bf16[128,4096]{1,0:T(8,128)(2,1)}, bf16[128,7168]{1,0:T(8,128)(2,1)}, bf16[896,4096]{1,0:T(8,128)(2,1)}, f32[1,128]{1,0:T(1,128)}) custom-call(bf16[128,4096]{1,0:T(8,128)(2,1)S(1)} %get-tuple-element.12.mixed_in, bf16[128,7168]{1,0:T(8,128)(2,1)S(1)} %get-tuple-element.13.hg_in, bf16[896,4096]{1,0:T(8,128)(2,1)S(1)} %get-tuple-element.14.wg_in, ...), custom_call_target="tpu_custom_call" | custom-call | tf_op jit(solution)/shard_map/finish/pallas_call | solution.py:603
